TPU v7x, 32 devices: a whole 2x2x4 slice. The times are simulated.
32 devices in a mesh: read: 8 (over z, core), tm: 4 (over y, x).
Axes of the slice: x: 2, y: 2, z: 4, core: 2. Of those that a mesh axis runs over, the one named last changes fastest.
Arguments:
- student_in: bfloat16 [8, 2048, 512], P('read', 'tm'), may hold values from -6 to 6
- teacher_rows: bfloat16 [8, 2048, 768], P('read', 'tm'), may hold values from -6 to 6
- valid: int32 [8], P('read'), may hold values from 512 to 2048, as said below
- conv_weight: bfloat16 [4, 3, 512, 512], replicated, may hold values from -0.15625 to 0.15625
- head_weight: bfloat16 [512, 5120], replicated, may hold values from -0.25 to 0.25
- teacher_head_weight: bfloat16 [768, 5120], replicated, may hold values from -0.21875 to 0.21875
Outputs:
- grad_conv: float32 [4, 3, 512, 512], P(None, None, 'read', 'tm')
- grad_head: float32 [512, 5120], P('read', 'tm')
Inputs may be any that keep to these rules, and one draw needn't show every extreme that they name: One read of each draw has all 2048 frames valid.
All inputs are finite; a program needn't handle non-finite values.
Results may differ from a plain program's by a relative error of at most 0.002.
Values may be sent and summed in bfloat16 or wider, within the bound.
A program may use at most 192 MiB of HBM per device.

v0:
```python
import math

import jax
import jax.numpy as jnp
from jax import lax
from jax.sharding import PartitionSpec as P

LAYERS = 4
BASE_DILATION = 32


def extended(x, sides, width):
    for axis, dim in sides:
        devices, length = (lax.axis_size(axis), x.shape[dim])
        up = [(i, (i + 1) % devices) for i in range(devices - 1)]
        down = [(j, i) for i, j in up]
        last = lax.slice_in_dim(x, length - width, length, axis=dim)
        leading = lax.slice_in_dim(x, 0, width, axis=dim)
        before = lax.ppermute(last, axis, up)
        after = lax.ppermute(leading, axis, down)
        x = jnp.concatenate([before, x, after], axis=dim)
    return x


def flatten(block):
    return block.reshape(-1, block.shape[-1])


def on_device(student_in, teacher_rows, valid, conv_weight, head_weight, teacher_head_weight):
    reads_dev, device_frames, width = student_in.shape
    scores = head_weight.shape[1]
    loss_scale = scores / (
        3.0 * math.sqrt(reads_dev * lax.axis_size("read") * device_frames * lax.axis_size("tm"))
    )
    first_frame = lax.axis_index("tm") * device_frames
    positions = first_frame + jnp.arange(device_frames, dtype=jnp.int32)
    signal_frame_mask = (positions[None, :] < valid[:, None]).astype(jnp.float32)[:, :, None]
    hidden = student_in
    saved = []
    for layer_number in range(LAYERS):
        receptive_reach = BASE_DILATION * 2**layer_number
        padded = extended(hidden, (("tm", 1),), receptive_reach)
        total = jnp.zeros((reads_dev * device_frames, width), jnp.float32)
        for tap_index in range(3):
            start = tap_index * receptive_reach
            total = total + jnp.dot(
                flatten(padded[:, start : start + device_frames]),
                conv_weight[layer_number, tap_index],
                preferred_element_type=jnp.float32,
            )
        pre = total.reshape(reads_dev, device_frames, width)
        saved.append((padded, pre, receptive_reach))
        hidden = (signal_frame_mask * (hidden.astype(jnp.float32) + jax.nn.silu(pre))).astype(
            jnp.bfloat16
        )
    flat_hidden = flatten(hidden)
    squash = jnp.tanh(jnp.dot(flat_hidden, head_weight, preferred_element_type=jnp.float32))
    student = 5.0 * squash
    teacher = 5.0 * jnp.tanh(
        jnp.dot(flatten(teacher_rows), teacher_head_weight, preferred_element_type=jnp.float32)
    )
    prob_teacher = jax.nn.softmax(teacher, axis=-1)
    prob_student = jax.nn.softmax(student, axis=-1)
    flat_mask = signal_frame_mask.reshape(-1, 1)
    g_score = (
        loss_scale * flat_mask * (prob_student - prob_teacher) * 5.0 * (1.0 - squash * squash)
    ).astype(jnp.bfloat16)
    head_part = jnp.dot(flat_hidden.T, g_score, preferred_element_type=jnp.float32)
    g_hidden = jnp.dot(g_score, head_weight.T, preferred_element_type=jnp.float32).reshape(
        reads_dev, device_frames, width
    )
    grads = []
    for layer_number in reversed(range(LAYERS)):
        padded, pre, receptive_reach = saved[layer_number]
        g_act = signal_frame_mask * g_hidden
        sigma = jax.nn.sigmoid(pre)
        g_pre = (g_act * sigma * (1.0 + pre * (1.0 - sigma))).astype(jnp.bfloat16)
        flat_pre = flatten(g_pre)
        taps = []
        for tap_index in range(3):
            start = tap_index * receptive_reach
            taps.append(
                jnp.dot(
                    flatten(padded[:, start : start + device_frames]).T,
                    flat_pre,
                    preferred_element_type=jnp.float32,
                )
            )
        grads.append(jnp.stack(taps))
        if layer_number > 0:
            g_padded = extended(g_pre, (("tm", 1),), receptive_reach)
            total = flatten(g_act)
            for tap_index in range(3):
                start = (2 - tap_index) * receptive_reach
                total = total + jnp.dot(
                    flatten(g_padded[:, start : start + device_frames]),
                    conv_weight[layer_number, tap_index].T,
                    preferred_element_type=jnp.float32,
                )
            g_hidden = total.reshape(reads_dev, device_frames, width)
    conv_part = jnp.stack(grads[::-1])
    conv_mid, head_mid = (
        lax.psum_scatter(conv_part, "read", scatter_dimension=2, tiled=True),
        lax.psum_scatter(head_part, "read", scatter_dimension=0, tiled=True),
    )
    grad_conv, grad_head = (
        lax.psum_scatter(conv_mid, "tm", scatter_dimension=3, tiled=True),
        lax.psum_scatter(head_mid, "tm", scatter_dimension=1, tiled=True),
    )
    return (grad_conv, grad_head)


def solution(mesh):
    return jax.shard_map(
        on_device,
        mesh=mesh,
        in_specs=(P("read", "tm", None), P("read", "tm", None), P("read"), P(), P(), P()),
        out_specs=(P(None, None, "read", "tm"), P("read", "tm")),
        check_vma=False,
    )
```

profile of v0, /device:TPU:0, one launch (start us, length us, event | category | flops | bytes accessed | tf_op | source)
XLA Modules:
  0.0 405.8 jit_solution(17656456900280934386)
XLA Ops:
  8.1 4.8 %collective-permute-start = (bf16[1,32,512]{2,1,0:T(8,128)(2,1)S(1)}, bf16[1,32,512]{2,1,0:T(8,128)(2,1)S(1)}, u32[]{:S(2)}, u32[]{:S(2)}) collective-permute-start(bf16[1,32,512]{2,1,0:T(8,128)(2,1)S(1)} %get-tuple-element.14), channel_id=1, source_target_pairs={{0,1},{1,2},{2,3},{4,5},{5,6},{6,7},{8,9},{9,10},{10,11},{12,13},{... | collective-permute-start | bytes 98312 | tf_op jit(solution)/shard_map/ppermute | solution.py:19
  14.9 2.6 fusion.91
  17.5 6.9 %fusion.1 = (f32[512]{0:T(512)S(1)}, f32[512,5120]{1,0:T(8,128)S(1)}) fusion(bf16[768,5120]{1,0:T(8,128)(2,1)} %param.11, bf16[1,512,768]{2,1,0:T(8,128)(2,1)S(1)} %copy-done), kind=kOutput, calls=%fused_computation.7 | convolution fusion | flops 4031774208 | bytes 19138560 | tf_op jit(solution)/shard_map/dot_general | solution.py:60
  24.4 3.0 fusion.2
  27.9 1.7 fusion.23
  31.3 5.2 %collective-permute-start.2 = (bf16[1,64,512]{2,1,0:T(8,128)(2,1)S(1)}, bf16[1,64,512]{2,1,0:T(8,128)(2,1)S(1)}, u32[]{:S(2)}, u32[]{:S(2)}) collective-permute-start(bf16[1,64,512]{2,1,0:T(8,128)(2,1)S(1)} %get-tuple-element.12), channel_id=1, source_target_pairs={{0,1},{1,2},{2,3},{4,5},{5,6},{6,7},{8,9},{9,10},{10,11},{12,13},{... | collective-permute-start | bytes 196616 | tf_op jit(solution)/shard_map/ppermute | solution.py:19
  38.4 1.7 fusion.21
  41.8 5.5 %collective-permute-start.4 = (bf16[1,128,512]{2,1,0:T(8,128)(2,1)S(1)}, bf16[1,128,512]{2,1,0:T(8,128)(2,1)S(1)}, u32[]{:S(2)}, u32[]{:S(2)}) collective-permute-start(bf16[1,128,512]{2,1,0:T(8,128)(2,1)S(1)} %get-tuple-element.10), channel_id=1, source_target_pairs={{0,1},{1,2},{2,3},{4,5},{5,6},{6,7},{8,9},{9,10},{10,11},{12,13},{... | collective-permute-start | bytes 393224 | tf_op jit(solution)/shard_map/ppermute | solution.py:19
  48.3 1.5 collective-permute-done.4
  49.8 1.7 fusion.19
  51.5 5.2 %collective-permute-start.6 = (bf16[1,256,512]{2,1,0:T(8,128)(2,1)S(1)}, bf16[1,256,512]{2,1,0:T(8,128)(2,1)S(1)}, u32[]{:S(2)}, u32[]{:S(2)}) collective-permute-start(bf16[1,256,512]{2,1,0:T(8,128)(2,1)S(1)} %get-tuple-element.8), channel_id=1, source_target_pairs={{0,1},{1,2},{2,3},{4,5},{5,6},{6,7},{8,9},{9,10},{10,11},{12,13},{... | collective-permute-start | bytes 786440 | tf_op jit(solution)/shard_map/ppermute | solution.py:19
  56.7 1.6 collective-permute-start.7
  58.7 9.7 %collective-permute-done.7 = bf16[1,256,512]{2,1,0:T(8,128)(2,1)S(1)} collective-permute-done((bf16[1,256,512]{2,1,0:T(8,128)(2,1)S(1)}, bf16[1,256,512]{2,1,0:T(8,128)(2,1)S(1)}, u32[]{:S(2)}, u32[]{:S(2)}) %collective-permute-start.7) | collective-permute-done | bytes 262176 | tf_op jit(solution)/shard_map/ppermute | solution.py:20
  70.4 3.3 multiply_reduce_fusion
  73.7 3.0 fusion
  76.7 8.6 %multiply_convert_fusion = bf16[512,5120]{1,0:T(8,128)(2,1)S(1)} fusion(f32[512,5120]{1,0:T(8,128)S(1)} %get-tuple-element.25, f32[512,5120]{1,0:T(8,128)S(1)} %get-tuple-element.23, f32[512]{0:T(512)S(1)} %fusion.2, f32[512]{0:T(512)S(1)} %get-tuple-element.22, f32[512]{0:T(512)S(1)} %fusion, f32[512]{0:T(512)S(1)} %get-tuple-element.24, f32[512]{0:T(512)S(1)} %fusion.133), kind=kLoop, calls=%fused_computation.1 | loop fusion | flops 34078720 | bytes 26224640 | tf_op jit(solution)/shard_map/convert_element_type | solution.py:67
  85.3 2.3 copy-done.2
  87.6 5.9 %fusion.52 = f32[512,5120]{1,0:T(8,128)} fusion(bf16[512,5120]{1,0:T(8,128)(2,1)S(1)} %multiply_convert_fusion, f32[512,512]{1,0:T(8,128)S(1)} %copy-done.5, bf16[1,512,512]{2,1,0:T(8,128)(2,1)S(1)} %get-tuple-element.20, f32[512]{0:T(512)S(1)} %fusion.134), kind=kOutput, calls=%fused_computation.104 | convolution fusion | flops 2686451712 | bytes 17303552 | tf_op jit(solution)/shard_map/dot_general | solution.py:68
  93.8 7.4 %multiply_convert_fusion.3 = (bf16[512,512]{1,0:T(8,128)(2,1)S(1)}, f32[512,512]{1,0:T(8,128)S(1)}) fusion(f32[512,512]{1,0:T(8,128)} %copy-done.4, bf16[512,5120]{1,0:T(8,128)(2,1)} %copy-done.2, bf16[512,5120]{1,0:T(8,128)(2,1)} %param.10, f32[512]{0:T(512)S(1)} %fusion.134), kind=kOutput, calls=%fused_computation.63 | convolution fusion | flops 2686976000 | bytes 13109248 | tf_op jit(solution)/shard_map/dot_general | solution.py:69
  101.2 3.8 collective-permute-start.9
  105.0 1.6 collective-permute-start.8
  109.6 4.7 %collective-permute-done.8 = bf16[1,256,512]{2,1,0:T(8,128)(2,1)S(1)} collective-permute-done((bf16[1,256,512]{2,1,0:T(8,128)(2,1)S(1)}, bf16[1,256,512]{2,1,0:T(8,128)(2,1)S(1)}, u32[]{:S(2)}, u32[]{:S(2)}) %collective-permute-start.8) | collective-permute-done | bytes 262176 | tf_op jit(solution)/shard_map/ppermute | solution.py:20
  115.5 2.1 collective-permute-start.11
  121.2 3.3 collective-permute-done.10
  125.8 2.8 collective-permute-start.13
  128.6 1.6 collective-permute-start.12
  132.4 2.4 collective-permute-done.12
  137.8 5.1 %pad_maximum_fusion = f32[4,3,512,512]{3,2,1,0:T(8,128)} fusion(f32[1,3,512,512]{3,2,1,0:T(8,128)S(1)} %maximum_bitcast_fusion.3, f32[1,3,512,512]{3,2,1,0:T(8,128)S(1)} %maximum_bitcast_fusion.2, f32[1,3,512,512]{3,2,1,0:T(8,128)S(1)} %maximum_bitcast_fusion.1, f32[1,3,512,512]{3,2,1,0:T(8,128)S(1)} %maximum_bitcast_fusion), kind=kLoop, calls=%fused_computation | loop fusion | flops 9437184 | bytes 25165824 | tf_op jit(solution)/shard_map/stack | solution.py:101
  143.0 60.8 %reduce-scatter.9.cloned.1.call-done = f32[64,5120]{1,0:T(8,128)} async-done(((f32[512,5120]{1,0:T(8,128)}), f32[64,5120]{1,0:T(8,128)}) %reduce-scatter.9.cloned.1.call-update) | async-done | bytes 1310736 | tf_op jit(solution)/shard_map/reduce_scatter | solution.py:104
  203.9 129.8 %reduce-scatter.5.cloned.1.call-done = f32[4,3,64,512]{3,2,1,0:T(8,128)} async-done(((f32[4,3,512,512]{3,2,1,0:T(8,128)}), f32[4,3,64,512]{3,2,1,0:T(8,128)}) %reduce-scatter.5.cloned.1.call-update) | async-done | bytes 1572880 | tf_op jit(solution)/shard_map/reduce_scatter | solution.py:103
  333.7 31.2 %reduce-scatter.11.cloned.1.call-done = f32[64,1280]{1,0:T(8,128)} async-done(((f32[64,5120]{1,0:T(8,128)}), f32[64,1280]{1,0:T(8,128)}) %reduce-scatter.11.cloned.1.call-update) | async-done | bytes 327696 | tf_op jit(solution)/shard_map/reduce_scatter | solution.py:108
  364.9 34.4 %reduce-scatter.7.cloned.1.call-done = f32[4,3,64,128]{3,2,1,0:T(8,128)} async-done(((f32[4,3,64,512]{3,2,1,0:T(8,128)}), f32[4,3,64,128]{3,2,1,0:T(8,128)}) %reduce-scatter.7.cloned.1.call-update) | async-done | bytes 393232 | tf_op jit(solution)/shard_map/reduce_scatter | solution.py:107
  (97 shorter events, 26.0 us)
Async XLA Ops:
  7.2 10.3 %copy-start = (bf16[1,512,768]{2,1,0:T(8,128)(2,1)S(1)}, bf16[1,512,768]{2,1,0:T(8,128)(2,1)}, u32[]{:S(2)}) copy-start(bf16[1,512,768]{2,1,0:T(8,128)(2,1)} %param.7) | copy-start | bytes 2359300
  7.2 196.6 %reduce-scatter.9.cloned.1.call-start = ((), (), s32[]{:S(2)}) async-start(), calls=%async_computation.6 | async-start | bytes 11796480 | tf_op jit(solution)/shard_map/reduce_scatter | solution.py:104
  8.1 19.8 %collective-permute-start = (bf16[1,32,512]{2,1,0:T(8,128)(2,1)S(1)}, bf16[1,32,512]{2,1,0:T(8,128)(2,1)S(1)}, u32[]{:S(2)}, u32[]{:S(2)}) collective-permute-start(bf16[1,32,512]{2,1,0:T(8,128)(2,1)S(1)} %get-tuple-element.14), channel_id=1, source_target_pairs={{0,1},{1,2},{2,3},{4,5},{5,6},{6,7},{8,9},{9,10},{10,11},{12,13},{... | collective-permute-start | bytes 98312 | tf_op jit(solution)/shard_map/ppermute | solution.py:19
  12.9 14.5 %collective-permute-start.1 = (bf16[1,32,512]{2,1,0:T(8,128)(2,1)S(1)}, bf16[1,32,512]{2,1,0:T(8,128)(2,1)S(1)}, u32[]{:S(2)}, u32[]{:S(2)}) collective-permute-start(bf16[1,32,512]{2,1,0:T(8,128)(2,1)S(1)} %get-tuple-element.15), channel_id=1, source_target_pairs={{1,0},{2,1},{3,2},{5,4},{6,5},{7,6},{9,8},{10,9},{11,10},{13,12},{... | collective-permute-start | bytes 98312 | tf_op jit(solution)/shard_map/ppermute | solution.py:20
  17.5 9.9 %slice-start = ((s8[6291456]{0:T(1024)(128)(4,1)}), s8[4194304]{0:T(1024)(128)(4,1)S(1)}, s32[]{:S(2)}) async-start(s8[6291456]{0:T(1024)(128)(4,1)} %bitcast.257), calls=%async_computation.8 | async-start | bytes 8388608
  17.5 9.9 %slice-start.1 = ((s8[6291456]{0:T(1024)(128)(4,1)}), s8[2097152]{0:T(1024)(128)(4,1)S(1)}, s32[]{:S(2)}) async-start(s8[6291456]{0:T(1024)(128)(4,1)} %bitcast.257), calls=%async_computation.9 | async-start | bytes 4194304
  24.4 3.0 copy-start.3
  24.4 3.5 copy-start.6
  29.5 6.9 %collective-permute-start.3 = (bf16[1,64,512]{2,1,0:T(8,128)(2,1)S(1)}, bf16[1,64,512]{2,1,0:T(8,128)(2,1)S(1)}, u32[]{:S(2)}, u32[]{:S(2)}) collective-permute-start(bf16[1,64,512]{2,1,0:T(8,128)(2,1)S(1)} %get-tuple-element.13), channel_id=1, source_target_pairs={{1,0},{2,1},{3,2},{5,4},{6,5},{7,6},{9,8},{10,9},{11,10},{13,12},{... | collective-permute-start | bytes 196616 | tf_op jit(solution)/shard_map/ppermute | solution.py:20
  31.3 7.1 %collective-permute-start.2 = (bf16[1,64,512]{2,1,0:T(8,128)(2,1)S(1)}, bf16[1,64,512]{2,1,0:T(8,128)(2,1)S(1)}, u32[]{:S(2)}, u32[]{:S(2)}) collective-permute-start(bf16[1,64,512]{2,1,0:T(8,128)(2,1)S(1)} %get-tuple-element.12), channel_id=1, source_target_pairs={{0,1},{1,2},{2,3},{4,5},{5,6},{6,7},{8,9},{9,10},{10,11},{12,13},{... | collective-permute-start | bytes 196616 | tf_op jit(solution)/shard_map/ppermute | solution.py:19
  40.1 7.8 %collective-permute-start.5 = (bf16[1,128,512]{2,1,0:T(8,128)(2,1)S(1)}, bf16[1,128,512]{2,1,0:T(8,128)(2,1)S(1)}, u32[]{:S(2)}, u32[]{:S(2)}) collective-permute-start(bf16[1,128,512]{2,1,0:T(8,128)(2,1)S(1)} %get-tuple-element.11), channel_id=1, source_target_pairs={{1,0},{2,1},{3,2},{5,4},{6,5},{7,6},{9,8},{10,9},{11,10},{13,12},{... | collective-permute-start | bytes 393224 | tf_op jit(solution)/shard_map/ppermute | solution.py:20
  41.8 8.0 %collective-permute-start.4 = (bf16[1,128,512]{2,1,0:T(8,128)(2,1)S(1)}, bf16[1,128,512]{2,1,0:T(8,128)(2,1)S(1)}, u32[]{:S(2)}, u32[]{:S(2)}) collective-permute-start(bf16[1,128,512]{2,1,0:T(8,128)(2,1)S(1)} %get-tuple-element.10), channel_id=1, source_target_pairs={{0,1},{1,2},{2,3},{4,5},{5,6},{6,7},{8,9},{9,10},{10,11},{12,13},{... | collective-permute-start | bytes 393224 | tf_op jit(solution)/shard_map/ppermute | solution.py:19
  49.8 20.7 %slice-start.4 = ((s8[5242880]{0:T(1024)(128)(4,1)}), s8[4194304]{0:T(1024)(128)(4,1)S(1)}, s32[]{:S(2)}) async-start(s8[5242880]{0:T(1024)(128)(4,1)} %bitcast.261), calls=%async_computation.12 | async-start | bytes 8388608
  51.5 17.4 %collective-permute-start.6 = (bf16[1,256,512]{2,1,0:T(8,128)(2,1)S(1)}, bf16[1,256,512]{2,1,0:T(8,128)(2,1)S(1)}, u32[]{:S(2)}, u32[]{:S(2)}) collective-permute-start(bf16[1,256,512]{2,1,0:T(8,128)(2,1)S(1)} %get-tuple-element.8), channel_id=1, source_target_pairs={{0,1},{1,2},{2,3},{4,5},{5,6},{6,7},{8,9},{9,10},{10,11},{12,13},{... | collective-permute-start | bytes 786440 | tf_op jit(solution)/shard_map/ppermute | solution.py:19
  56.6 13.8 %slice-start.5 = ((s8[5242880]{0:T(1024)(128)(4,1)}), s8[1048576]{0:T(1024)(128)(4,1)S(1)}, s32[]{:S(2)}) async-start(s8[5242880]{0:T(1024)(128)(4,1)} %bitcast.261), calls=%async_computation.13 | async-start | bytes 2097152
  56.7 11.8 %collective-permute-start.7 = (bf16[1,256,512]{2,1,0:T(8,128)(2,1)S(1)}, bf16[1,256,512]{2,1,0:T(8,128)(2,1)S(1)}, u32[]{:S(2)}, u32[]{:S(2)}) collective-permute-start(bf16[1,256,512]{2,1,0:T(8,128)(2,1)S(1)} %get-tuple-element.9), channel_id=1, source_target_pairs={{1,0},{2,1},{3,2},{5,4},{6,5},{7,6},{9,8},{10,9},{11,10},{13,12},{... | collective-permute-start | bytes 786440 | tf_op jit(solution)/shard_map/ppermute | solution.py:20
  76.7 10.9 %copy-start.5 = (f32[512,512]{1,0:T(8,128)S(1)}, f32[512,512]{1,0:T(8,128)}, u32[]{:S(2)}) copy-start(f32[512,512]{1,0:T(8,128)} %copy-done.4) | copy-start | bytes 3145732
  85.3 2.3 copy-start.2
  93.5 240.2 %reduce-scatter.5.cloned.1.call-start = ((), (), s32[]{:S(2)}) async-start(), calls=%async_computation.4 | async-start | bytes 14155776 | tf_op jit(solution)/shard_map/reduce_scatter | solution.py:103
  101.2 13.6 %collective-permute-start.9 = (bf16[1,256,512]{2,1,0:T(8,128)(2,1)S(1)}, bf16[1,256,512]{2,1,0:T(8,128)(2,1)S(1)}, u32[]{:S(2)}, u32[]{:S(2)}) collective-permute-start(bf16[1,256,512]{2,1,0:T(8,128)(2,1)S(1)} %get-tuple-element.6), channel_id=1, source_target_pairs={{0,1},{1,2},{2,3},{4,5},{5,6},{6,7},{8,9},{9,10},{10,11},{12,13},{... | collective-permute-start | bytes 786440 | tf_op jit(solution)/shard_map/ppermute | solution.py:19
  105.0 3.3 slice-start.2
  105.0 9.3 %collective-permute-start.8 = (bf16[1,256,512]{2,1,0:T(8,128)(2,1)S(1)}, bf16[1,256,512]{2,1,0:T(8,128)(2,1)S(1)}, u32[]{:S(2)}, u32[]{:S(2)}) collective-permute-start(bf16[1,256,512]{2,1,0:T(8,128)(2,1)S(1)} %get-tuple-element.7), channel_id=1, source_target_pairs={{1,0},{2,1},{3,2},{5,4},{6,5},{7,6},{9,8},{10,9},{11,10},{13,12},{... | collective-permute-start | bytes 786440 | tf_op jit(solution)/shard_map/ppermute | solution.py:20
  108.0 6.8 %copy-start.7 = (f32[512,512]{1,0:T(8,128)S(1)}, f32[512,512]{1,0:T(8,128)}, u32[]{:S(2)}) copy-start(f32[512,512]{1,0:T(8,128)} %get-tuple-element.21) | copy-start | bytes 3145732
  115.5 9.5 %collective-permute-start.11 = (bf16[1,128,512]{2,1,0:T(8,128)(2,1)S(1)}, bf16[1,128,512]{2,1,0:T(8,128)(2,1)S(1)}, u32[]{:S(2)}, u32[]{:S(2)}) collective-permute-start(bf16[1,128,512]{2,1,0:T(8,128)(2,1)S(1)} %get-tuple-element.4), channel_id=1, source_target_pairs={{0,1},{1,2},{2,3},{4,5},{5,6},{6,7},{8,9},{9,10},{10,11},{12,13},{... | collective-permute-start | bytes 393224 | tf_op jit(solution)/shard_map/ppermute | solution.py:19
  117.7 6.9 %collective-permute-start.10 = (bf16[1,128,512]{2,1,0:T(8,128)(2,1)S(1)}, bf16[1,128,512]{2,1,0:T(8,128)(2,1)S(1)}, u32[]{:S(2)}, u32[]{:S(2)}) collective-permute-start(bf16[1,128,512]{2,1,0:T(8,128)(2,1)S(1)} %get-tuple-element.5), channel_id=1, source_target_pairs={{1,0},{2,1},{3,2},{5,4},{6,5},{7,6},{9,8},{10,9},{11,10},{13,12},{... | collective-permute-start | bytes 393224 | tf_op jit(solution)/shard_map/ppermute | solution.py:20
  120.4 4.6 %copy-start.8 = (f32[512,512]{1,0:T(8,128)S(1)}, f32[512,512]{1,0:T(8,128)}, u32[]{:S(2)}) copy-start(f32[512,512]{1,0:T(8,128)} %get-tuple-element.19) | copy-start | bytes 3145732
  125.8 9.5 %collective-permute-start.13 = (bf16[1,64,512]{2,1,0:T(8,128)(2,1)S(1)}, bf16[1,64,512]{2,1,0:T(8,128)(2,1)S(1)}, u32[]{:S(2)}, u32[]{:S(2)}) collective-permute-start(bf16[1,64,512]{2,1,0:T(8,128)(2,1)S(1)} %get-tuple-element.2), channel_id=1, source_target_pairs={{0,1},{1,2},{2,3},{4,5},{5,6},{6,7},{8,9},{9,10},{10,11},{12,13},{... | collective-permute-start | bytes 196616 | tf_op jit(solution)/shard_map/ppermute | solution.py:19
  128.6 6.2 %collective-permute-start.12 = (bf16[1,64,512]{2,1,0:T(8,128)(2,1)S(1)}, bf16[1,64,512]{2,1,0:T(8,128)(2,1)S(1)}, u32[]{:S(2)}, u32[]{:S(2)}) collective-permute-start(bf16[1,64,512]{2,1,0:T(8,128)(2,1)S(1)} %get-tuple-element.3), channel_id=1, source_target_pairs={{1,0},{2,1},{3,2},{5,4},{6,5},{7,6},{9,8},{10,9},{11,10},{13,12},{... | collective-permute-start | bytes 196616 | tf_op jit(solution)/shard_map/ppermute | solution.py:20
  131.6 3.7 copy-start.9
  142.9 256.4 %copy-start.1 = (bf16[1,512,768]{2,1,0:T(8,128)(2,1)S(1)}, bf16[1,512,768]{2,1,0:T(8,128)(2,1)}, u32[]{:S(2)}) copy-start(bf16[1,512,768]{2,1,0:T(8,128)(2,1)} %param.7) | copy-start | bytes 2359300
  142.9 222.0 %reduce-scatter.11.cloned.1.call-start = ((), (), s32[]{:S(2)}) async-start(), calls=%async_computation.7 | async-start | bytes 1638400 | tf_op jit(solution)/shard_map/reduce_scatter | solution.py:108
  203.8 195.5 %reduce-scatter.7.cloned.1.call-start = ((), (), s32[]{:S(2)}) async-start(), calls=%async_computation.5 | async-start | bytes 1966080 | tf_op jit(solution)/shard_map/reduce_scatter | solution.py:107
  (2 other events, 2.7 us)
Sparse Core Ops, SparseCore 0:
  93.6 110.1 reduce-scatter.8
  206.1 127.5 reduce-scatter.4
  337.2 27.6 reduce-scatter.10
  368.3 30.8 reduce-scatter.6
where the time goes:
time: 406 us
  waiting for transfers between devices  280 us (69%)
  matrix products  45.2 us (11%)
  starting transfers between devices  39.7 us (10%)
  other arithmetic  20.8 us (5%)
  between operations  15 us (4%)
  local copies, waits for them, and re-layouts  5.23 us (1%)
    reduce_scatter x1, waiting for transfers between devices, on_device(): lax.psum_scatter(conv_part, 'read', scatter_dimension=2, tiled=True)  130 us
    reduce_scatter x1, waiting for transfers between devices, on_device(): lax.psum_scatter(head_part, 'read', scatter_dimension=0, tiled=True)  60.8 us
    reduce_scatter x1, waiting for transfers between devices, on_device(): lax.psum_scatter(conv_mid, 'tm', scatter_dimension=3, tiled=True)  34.4 us
    reduce_scatter x1, waiting for transfers between devices, on_device(): lax.psum_scatter(head_mid, 'tm', scatter_dimension=1, tiled=True)  31.2 us
    ppermute x7, starting transfers between devices, extended(): before = lax.ppermute(last, axis, up)  29.4 us
    ppermute x7, waiting for transfers between devices, extended(): after = lax.ppermute(leading, axis, down)  20.7 us
    dot_general x12, matrix products, on_device(): jnp.dot(flatten(padded[:, start:start + device_frames]), conv_weight[laye...  11.1 us
    ppermute x7, starting transfers between devices, extended(): after = lax.ppermute(leading, axis, down)  9.88 us
  transfers between devices with their start and end apart: 18, of which 11 were waited for; matrix products, arithmetic and copies ran while one was open for 10% of the time, Pallas kernels for 0%

commit v1 on v0

v1 whole, which is shorter than its diff:
```python
import functools
import math

import jax
import jax.numpy as jnp
from jax import lax
from jax.experimental import pallas as pl
from jax.experimental.pallas import tpu as pltpu
from jax.sharding import PartitionSpec as P

LAYERS = 4
BASE_DILATION = 32
HEAD_GROUPS = 5
MESH = pl.DeviceIdType.MESH
BF16, F32 = jnp.bfloat16, jnp.float32


def reach(layer):
    return BASE_DILATION * 2**layer


def extended(x, width):
    devices, length = (lax.axis_size("tm"), x.shape[0])
    up = [(i, (i + 1) % devices) for i in range(devices - 1)]
    down = [(j, i) for i, j in up]
    before = lax.ppermute(x[length - width :], "tm", up)
    after = lax.ppermute(x[:width], "tm", down)
    return jnp.concatenate([before, x, after], axis=0)


def dot_tn(a, b):
    return lax.dot_general(a, b, (((0,), (0,)), ((), ())), preferred_element_type=F32)


def dot_nt(a, b):
    return lax.dot_general(a, b, (((1,), (1,)), ((), ())), preferred_element_type=F32)


def backward_kernel(
    n_read,
    n_tm,
    hid_mine,
    hid_other,
    gs,
    hw,
    cw,
    pre0,
    pre1,
    pre2,
    pre3,
    mask,
    out_conv,
    out_head,
    hid_far,
    gs_far,
    grad,
    gpad0,
    gpad1,
    gpad2,
    gpad3,
    gp_far,
    send_h,
    recv_h,
    acc_h,
    last_h,
    send_c,
    recv_c,
    acc_c,
    last_c,
    hid_sem,
    gs_sem,
    gp_sem,
    halo_sem,
    two_sem,
    three_sem,
):
    pres = (pre0, pre1, pre2, pre3)
    gpads = (gpad0, gpad1, gpad2, gpad3)
    frames, scores = gs.shape
    width = cw.shape[-1]
    n_q = n_read // 2
    half = width // 2
    rows = width // n_read
    cols = scores // n_tm
    conv_cols = width // n_tm
    sub = cols // HEAD_GROUPS
    r, t = lax.axis_index("read"), lax.axis_index("tm")
    core, q = lax.rem(r, 2), r // 2
    twin = {"read": 2 * q + 1 - core}
    tm_peers = [{"tm": lax.rem(t + k, n_tm)} for k in range(1, n_tm)]
    q_next = [lax.rem(q + k, n_q) for k in range(1, n_q)]
    q_peers = [{"read": 2 * other + core} for other in q_next]

    barrier = pltpu.get_barrier_semaphore()
    peers = [twin] + tm_peers + q_peers
    for peer in peers:
        pl.semaphore_signal(barrier, inc=1, device_id=peer, device_id_type=MESH)
    pl.semaphore_wait(barrier, len(peers))

    sent = []

    def remote(src, dst, send_sem, recv_sem, peer):
        return pltpu.make_async_remote_copy(
            src_ref=src,
            dst_ref=dst,
            send_sem=send_sem,
            recv_sem=recv_sem,
            device_id=peer,
            device_id_type=MESH,
        )

    def start(*what):
        copy = remote(*what)
        copy.start()
        sent.append(copy)
        return copy

    hid_copy = start(hid_other, hid_far, hid_sem.at[0], hid_sem.at[1], twin)
    gs_copies = []
    for s in range(HEAD_GROUPS):
        for owner in range(n_tm):
            part = pl.ds(owner * cols + s * sub, sub)
            gs_copies.append(
                start(
                    gs.at[:, part],
                    gs_far.at[:, part],
                    gs_sem.at[0, s, owner],
                    gs_sem.at[1, s, owner],
                    twin,
                )
            )

    step = scores // HEAD_GROUPS
    for s in range(HEAD_GROUPS):
        part = dot_nt(gs[:, s * step : (s + 1) * step], hw[:, s * step : (s + 1) * step])
        grad[...] = part if s == 0 else grad[...] + part

    gp_copies = {}
    two = {}
    three = {}
    halos = {}

    def make_gpre(layer):
        d = reach(layer)
        gpad, pre = gpads[layer], pres[layer][...]
        sigma = 1.0 / (1.0 + jnp.exp(-pre))
        g_act = mask[...] * grad[...]
        grad[...] = g_act
        gpad[d : d + frames, :] = (g_act * sigma * (1.0 + pre * (1.0 - sigma))).astype(BF16)
        if layer > 0:
            before = remote(
                gpad.at[pl.ds(d, d)],
                gpad.at[pl.ds(d + frames, d)],
                halo_sem.at[0, 0, layer],
                halo_sem.at[0, 1, layer],
                {"tm": lax.rem(t + n_tm - 1, n_tm)},
            )
            after = remote(
                gpad.at[pl.ds(frames, d)],
                gpad.at[pl.ds(0, d)],
                halo_sem.at[1, 0, layer],
                halo_sem.at[1, 1, layer],
                {"tm": lax.rem(t + 1, n_tm)},
            )
            halos[layer] = (before, after)

            @pl.when(t > 0)
            def _():
                before.start()

            @pl.when(t < n_tm - 1)
            def _():
                after.start()

            @pl.when(t == 0)
            def _():
                gpad[0:d, :] = jnp.zeros((d, width), BF16)

            @pl.when(t == n_tm - 1)
            def _():
                gpad[d + frames : d + frames + d, :] = jnp.zeros((d, width), BF16)

        gp_copies[layer] = start(
            gpad.at[pl.ds(d, frames)],
            gp_far.at[layer],
            gp_sem.at[0, layer],
            gp_sem.at[1, layer],
            twin,
        )

    def back(layer):
        d = reach(layer)
        gpad = gpads[layer]
        grad[...] = grad[...] + dot_nt(gpad[d : d + frames, :], cw[layer, 1])
        before, after = halos[layer]

        @pl.when(t < n_tm - 1)
        def _():
            before.wait_recv()

        @pl.when(t > 0)
        def _():
            after.wait_recv()

        grad[...] = grad[...] + dot_nt(gpad[2 * d : 2 * d + frames, :], cw[layer, 0])
        grad[...] = grad[...] + dot_nt(gpad[0:frames, :], cw[layer, 2])

        @pl.when(t > 0)
        def _():
            before.wait_send()

        @pl.when(t < n_tm - 1)
        def _():
            after.wait_send()

    def send_two(group, send_ref, recv_ref):
        two[group] = [
            start(
                send_ref.at[lax.rem(t + k, n_tm)],
                recv_ref.at[k - 1],
                two_sem.at[0, group, k - 1],
                two_sem.at[1, group, k - 1],
                tm_peers[k - 1],
            )
            for k in range(1, n_tm)
        ]

    hid_rows = sum(frames + 2 * reach(l) for l in range(LAYERS))

    def head(s):
        for owner in range(n_tm):
            gs_copies[s * n_tm + owner].wait_recv()
            at = owner * cols + s * sub
            total = dot_tn(hid_mine[hid_rows : hid_rows + frames, :], gs[:, at : at + sub])
            total = total + dot_tn(hid_far[hid_rows : hid_rows + frames, :], gs_far[:, at : at + sub])
            send_h[s, owner] = total.astype(BF16)

            @pl.when(t == owner)
            def _():
                acc_h[s] = total

        send_two(LAYERS + s, send_h.at[s], recv_h.at[s])

    def conv(layer):
        gp_copies[layer].wait_recv()
        d = reach(layer)
        base = sum(frames + 2 * reach(l) for l in range(layer))
        for k in range(3):
            at = base + k * d
            total = dot_tn(hid_mine[at : at + frames, :], gpads[layer][d : d + frames, :])
            total = total + dot_tn(hid_far[at : at + frames, :], gp_far[layer])
            for owner in range(n_tm):
                chunk = total[:, owner * conv_cols : (owner + 1) * conv_cols]
                send_c[layer, owner, k] = chunk.astype(BF16)

                @pl.when(t == owner)
                def _():
                    acc_c[layer, k] = chunk

        send_two(layer, send_c.at[layer], recv_c.at[layer])

    def finish_two(group):
        for copy in two[group]:
            copy.wait_recv()
        if group < LAYERS:
            for k in range(3):
                total = acc_c[group, k]
                for slot in range(n_tm - 1):
                    total = total + recv_c[group, slot, k].astype(F32)
                acc_c[group, k] = total
        else:
            total = acc_h[group - LAYERS]
            for slot in range(n_tm - 1):
                total = total + recv_h[group - LAYERS, slot].astype(F32)
            acc_h[group - LAYERS] = total
        three[group] = []
        for k in range(1, n_q):
            part = pl.ds(pl.multiple_of(q_next[k - 1] * rows, rows), rows)
            if group < LAYERS:
                src, dst = acc_c.at[group, :, part], last_c.at[group, k - 1]
            else:
                src, dst = acc_h.at[group - LAYERS, part], last_h.at[group - LAYERS, k - 1]
            three[group].append(
                start(
                    src,
                    dst,
                    three_sem.at[0, group, k - 1],
                    three_sem.at[1, group, k - 1],
                    q_peers[k - 1],
                )
            )

    def finish_three(group):
        for copy in three[group]:
            copy.wait_recv()
        part = pl.ds(pl.multiple_of(q * rows, rows), rows)
        if group < LAYERS:
            for k in range(3):
                total = acc_c[group, k, part, :]
                for slot in range(n_q - 1):
                    total = total + last_c[group, slot, k]
                out_conv[group, k] = total
        else:
            s = group - LAYERS
            total = acc_h[s, part, :]
            for slot in range(n_q - 1):
                total = total + last_h[s, slot]
            out_head[:, s * sub : (s + 1) * sub] = total

    make_gpre(3)
    hid_copy.wait_recv()
    head(0)
    head(1)
    back(3)
    make_gpre(2)
    head(2)
    head(3)
    back(2)
    make_gpre(1)
    head(4)
    conv(3)
    finish_two(4)
    back(1)
    make_gpre(0)
    conv(2)
    finish_two(5)
    conv(1)
    finish_two(6)
    conv(0)
    finish_two(7)
    finish_two(8)
    finish_three(4)
    finish_two(3)
    finish_three(5)
    finish_two(2)
    finish_three(6)
    finish_three(7)
    finish_two(1)
    finish_three(8)
    finish_two(0)
    for group in (3, 2, 1, 0):
        finish_three(group)
    for copy in sent:
        copy.wait_send()


def backward(hid_mine, hid_other, gs, hw, cw, pres, mask):
    n_read, n_tm = lax.axis_size("read"), lax.axis_size("tm")
    frames, scores = gs.shape
    width = cw.shape[-1]
    n_q, half, rows = n_read // 2, width // 2, width // n_read
    cols, conv_cols = scores // n_tm, width // n_tm
    sub = cols // HEAD_GROUPS
    groups = LAYERS + HEAD_GROUPS
    vmem = pl.BlockSpec(memory_space=pltpu.VMEM)
    dma = pltpu.SemaphoreType.DMA
    return pl.pallas_call(
        functools.partial(backward_kernel, n_read, n_tm),
        out_shape=(
            jax.ShapeDtypeStruct((LAYERS, 3, rows, conv_cols), F32),
            jax.ShapeDtypeStruct((rows, cols), F32),
        ),
        in_specs=[vmem] * 10,
        out_specs=(vmem, vmem),
        scratch_shapes=[
            pltpu.VMEM(hid_mine.shape, BF16),
            pltpu.VMEM((frames, scores), BF16),
            pltpu.VMEM((frames, width), F32),
        ]
        + [pltpu.VMEM((frames + 2 * reach(l), width), BF16) for l in range(LAYERS)]
        + [
            pltpu.VMEM((LAYERS, frames, width), BF16),
            pltpu.VMEM((HEAD_GROUPS, n_tm, half, sub), BF16),
            pltpu.VMEM((HEAD_GROUPS, n_tm - 1, half, sub), BF16),
            pltpu.VMEM((HEAD_GROUPS, half, sub), F32),
            pltpu.VMEM((HEAD_GROUPS, n_q - 1, rows, sub), F32),
            pltpu.VMEM((LAYERS, n_tm, 3, half, conv_cols), BF16),
            pltpu.VMEM((LAYERS, n_tm - 1, 3, half, conv_cols), BF16),
            pltpu.VMEM((LAYERS, 3, half, conv_cols), F32),
            pltpu.VMEM((LAYERS, n_q - 1, 3, rows, conv_cols), F32),
            dma((2,)),
            dma((2, HEAD_GROUPS, n_tm)),
            dma((2, LAYERS)),
            dma((2, 2, LAYERS)),
            dma((2, groups, n_tm - 1)),
            dma((2, groups, n_q - 1)),
        ],
        compiler_params=pltpu.CompilerParams(
            collective_id=1, has_side_effects=True, vmem_limit_bytes=60 * 2**20
        ),
    )(hid_mine, hid_other, gs, hw, cw, *pres, mask)


def on_device(student_in, teacher_rows, valid, conv_weight, head_weight, teacher_head_weight):
    reads_dev, frames, width = student_in.shape
    n_read = lax.axis_size("read")
    scores = head_weight.shape[1]
    loss_scale = scores / (
        3.0 * math.sqrt(reads_dev * n_read * frames * lax.axis_size("tm"))
    )
    first_frame = lax.axis_index("tm") * frames
    positions = first_frame + jnp.arange(frames, dtype=jnp.int32)
    mask = (positions < valid[0]).astype(F32)[:, None]
    hidden = student_in[0]
    pads, pres = [], []
    for layer in range(LAYERS):
        d = reach(layer)
        padded = extended(hidden, d)
        pre = jnp.zeros((frames, width), F32)
        for k in range(3):
            pre = pre + jnp.dot(
                padded[k * d : k * d + frames], conv_weight[layer, k], preferred_element_type=F32
            )
        pads.append(padded)
        pres.append(pre)
        hidden = (mask * (hidden.astype(F32) + jax.nn.silu(pre))).astype(BF16)
    squash = jnp.tanh(jnp.dot(hidden, head_weight, preferred_element_type=F32))
    teacher = 5.0 * jnp.tanh(
        jnp.dot(teacher_rows[0], teacher_head_weight, preferred_element_type=F32)
    )
    prob_teacher = jax.nn.softmax(teacher, axis=-1)
    prob_student = jax.nn.softmax(5.0 * squash, axis=-1)
    g_score = (
        loss_scale * mask * (prob_student - prob_teacher) * 5.0 * (1.0 - squash * squash)
    ).astype(BF16)
    every = jnp.concatenate(pads + [hidden], axis=0)
    every = every.reshape(every.shape[0], n_read // 2, 2, width // n_read)
    core = lax.rem(lax.axis_index("read"), 2)
    mine, other = (
        lax.dynamic_index_in_dim(every, which, 2, keepdims=False).reshape(-1, width // 2)
        for which in (core, 1 - core)
    )
    return backward(mine, other, g_score, head_weight, conv_weight, pres, mask)


def solution(mesh):
    return jax.shard_map(
        on_device,
        mesh=mesh,
        in_specs=(P("read", "tm", None), P("read", "tm", None), P("read"), P(), P(), P()),
        out_specs=(P(None, None, "read", "tm"), P("read", "tm")),
        check_vma=False,
    )
```

time: 406 us -> 246 us (0.61)
  waiting for transfers between devices: 280 us -> 0.66 us
  Pallas kernels: 0 us -> 119 us
  local copies, waits for them, and re-layouts: 5.23 us -> 32.7 us
  between operations: 15 us -> 1.56 us
  starting transfers between devices: 39.7 us -> 27.7 us
  matrix products: 45.2 us -> 39.1 us
    reduce_scatter x4 -> x0, waiting for transfers between devices: 256 us -> none  [the longest x1 130 us: on_device(): lax.psum_scatter(conv_part, 'read', scatter_dimension=2, tiled=True)]
    pallas_call x0 -> x1, Pallas kernels: none -> 119 us  [backward(): pl.pallas_call(functools.partial(backward_kernel, n_read, n_tm), out_shap...]
    ppermute x14 -> x8, waiting for transfers between devices: 23.6 us -> 0.66 us  [the longest x4 0.65 us: extended(): after = lax.ppermute(x[:width], 'tm', down)]
    ppermute x14 -> x8, starting transfers between devices: 39.3 us -> 27.7 us  [the longest x4 22.6 us: extended(): before = lax.ppermute(x[length - width:], 'tm', up)]
    concatenate x0 -> x5, local copies, waits for them, and re-layouts: none -> 10.1 us  [on_device(): every = jnp.concatenate(pads + [hidden], axis=0)]
    another operation x5 -> x0, other arithmetic: 6.37 us -> none  [on_device(): conv_part = jnp.stack(grads[::-1])]
    dot_general x37 -> x14, matrix products: 45.2 us -> 39.1 us  [the longest x12 24.4 us: on_device(): jnp.dot(padded[k * d:k * d + frames], conv_weight[layer, k], preferred_el...]
    reshape x0 -> x2, local copies, waits for them, and re-layouts: none -> 6.04 us  [on_device(): lax.dynamic_index_in_dim(every, which, 2, keepdims=False)]
  transfers between devices with their start and end apart: 18 -> 8, of which waited for: 11 -> 1; matrix products, arithmetic and copies ran while one was open for 10% -> 12% of each run, Pallas kernels for 0% -> 0%
where the time goes in v1:
time: 246 us; the launch traced here: 245 us
  Pallas kernels  119 us (48%)
  matrix products  39.1 us (16%)
  local copies, waits for them, and re-layouts  32.7 us (13%)
  starting transfers between devices  27.7 us (11%)
  other arithmetic  23.7 us (10%)
    pallas_call x1, Pallas kernels, backward(): pl.pallas_call(functools.partial(backward_kernel, n_read, n_tm), out_shap...  119 us
    dot_general x12, matrix products, on_device(): jnp.dot(padded[k * d:k * d + frames], conv_weight[layer, k], preferred_el...  24.4 us
    ppermute x4, starting transfers between devices, extended(): before = lax.ppermute(x[length - width:], 'tm', up)  22.6 us
    convert_element_type x1, other arithmetic, on_device(): g_score = (loss_scale * mask * (prob_student - prob_teacher) * 5.0 * (1.0...  13 us
    concatenate x5, local copies, waits for them, and re-layouts, on_device(): every = jnp.concatenate(pads + [hidden], axis=0)  10.1 us
    dot_general x1, matrix products, on_device(): squash = jnp.tanh(jnp.dot(hidden, head_weight, preferred_element_type=F32))  8.04 us
    unnamed x15, local copies, waits for them, and re-layouts  7.73 us
    reduce_sum x1, other arithmetic, on_device(): prob_student = jax.nn.softmax(5.0 * squash, axis=-1)  6.92 us
  transfers between devices with their start and end apart: 8, of which 1 were waited for; matrix products, arithmetic and copies ran while one was open for 12% of the time, Pallas kernels for 0%

profile of v1, /device:TPU:0, one launch (start us, length us, event | category | flops | bytes accessed | tf_op | source)
XLA Modules:
  0.0 244.7 jit_solution(9720412801698269897)
XLA Ops:
  2.8 5.5 %collective-permute-start = (bf16[32,512]{1,0:T(8,128)(2,1)S(1)}, bf16[32,512]{1,0:T(8,128)(2,1)S(1)}, u32[]{:S(2)}, u32[]{:S(2)}) collective-permute-start(bf16[32,512]{1,0:T(8,128)(2,1)S(1)} %get-tuple-element.11), channel_id=1, source_target_pairs={{0,1},{1,2},{2,3},{4,5},{5,6},{6,7},{8,9},{9,10},{10,11},{12,13},{... | collective-permute-start | bytes 98312 | tf_op jit(solution)/shard_map/ppermute | solution.py:26
  8.9 1.6 fusion.34
  11.3 6.7 %fusion.1 = (f32[512]{0:T(512)S(1)}, f32[512,5120]{1,0:T(8,128)S(1)}) fusion(bf16[768,5120]{1,0:T(8,128)(2,1)} %param.11, bf16[1,512,768]{2,1,0:T(8,128)(2,1)S(1)} %copy-done), kind=kOutput, calls=%fused_computation.6 | convolution fusion | flops 4031774208 | bytes 19138560 | tf_op jit(solution)/shard_map/dot_general | solution.py:419
  18.1 4.0 %copy-done.2 = f32[512,5120]{1,0:T(8,128)} copy-done((f32[512,5120]{1,0:T(8,128)}, f32[512,5120]{1,0:T(8,128)S(1)}, u32[]{:S(2)}) %copy-start.2) | copy-done | bytes 10485784
  22.1 2.9 %fusion.2 = f32[512]{0:T(512)S(1)} fusion(f32[512,5120]{1,0:T(8,128)S(1)} %get-tuple-element.21, f32[512]{0:T(512)S(1)} %get-tuple-element.20), kind=kLoop, calls=%fused_computation.7 | loop fusion | flops 7863808 | bytes 10489856 | tf_op jit(solution)/shard_map/reduce_sum | solution.py:421
  25.3 1.5 fusion.18
  26.8 2.7 %multiply_convert_fusion.4 = (bf16[512,512]{1,0:T(8,128)(2,1)S(1)}, f32[512,512]{1,0:T(8,128)}) fusion(f32[512]{0:T(512)S(1)} %fusion.51, bf16[1,512,512]{2,1,0:T(8,128)(2,1)S(1)} %copy-done.3, f32[512,512]{1,0:T(8,128)S(1)} %fusion.18, f32[512,512]{1,0:T(8,128)S(1)} %fusion.34, bf16[4,3,512,512]{3,2,1,0:T(8,128)(2,1)} %cw.1, ...), kind=kOutput, calls=%fused_computation.19 | convolution fusion | flops 272105472 | bytes 5277696 | tf_op jit(solution)/shard_map/dot_general | solution.py:411
  29.5 1.3 collective-permute-start.3
  30.8 1.5 fusion.30
  32.5 5.5 %collective-permute-start.2 = (bf16[64,512]{1,0:T(8,128)(2,1)S(1)}, bf16[64,512]{1,0:T(8,128)(2,1)S(1)}, u32[]{:S(2)}, u32[]{:S(2)}) collective-permute-start(bf16[64,512]{1,0:T(8,128)(2,1)S(1)} %get-tuple-element.9), channel_id=1, source_target_pairs={{0,1},{1,2},{2,3},{4,5},{5,6},{6,7},{8,9},{9,10},{10,11},{12,13},{... | collective-permute-start | bytes 196616 | tf_op jit(solution)/shard_map/ppermute | solution.py:26
  38.9 1.5 copy.76
  40.4 1.5 fusion.15
  41.9 2.7 %multiply_convert_fusion.3 = (bf16[512,512]{1,0:T(8,128)(2,1)S(1)}, f32[512,512]{1,0:T(8,128)}) fusion(bf16[512,512]{1,0:T(8,128)(2,1)S(1)} %get-tuple-element.12, f32[512]{0:T(512)S(1)} %fusion.51, f32[512,512]{1,0:T(8,128)S(1)} %fusion.15, f32[512,512]{1,0:T(8,128)S(1)} %fusion.30, bf16[4,3,512,512]{3,2,1,0:T(8,128)(2,1)} %cw.1, ...), kind=kOutput, calls=%fused_computation.18 | convolution fusion | flops 272105472 | bytes 5310464 | tf_op jit(solution)/shard_map/dot_general | solution.py:411
  45.9 2.5 %fusion.26 = f32[512,512]{1,0:T(8,128)} fusion(bf16[512,512]{1,0:T(8,128)(2,1)S(1)} %get-tuple-element.14, bf16[4,3,512,512]{3,2,1,0:T(8,128)(2,1)} %cw.1), kind=kOutput, calls=%fused_computation.47 | convolution fusion | flops 268435456 | bytes 2097152 | tf_op jit(solution)/shard_map/dot_general | solution.py:411
  48.7 5.5 %collective-permute-start.4 = (bf16[128,512]{1,0:T(8,128)(2,1)S(1)}, bf16[128,512]{1,0:T(8,128)(2,1)S(1)}, u32[]{:S(2)}, u32[]{:S(2)}) collective-permute-start(bf16[128,512]{1,0:T(8,128)(2,1)S(1)} %get-tuple-element.7), channel_id=1, source_target_pairs={{0,1},{1,2},{2,3},{4,5},{5,6},{6,7},{8,9},{9,10},{10,11},{12,13},{... | collective-permute-start | bytes 393224 | tf_op jit(solution)/shard_map/ppermute | solution.py:26
  55.7 1.5 fusion.12
  57.2 3.1 %multiply_convert_fusion.2 = (bf16[512,512]{1,0:T(8,128)(2,1)S(1)}, f32[512,512]{1,0:T(8,128)}) fusion(bf16[512,512]{1,0:T(8,128)(2,1)S(1)} %get-tuple-element.14, f32[512]{0:T(512)S(1)} %fusion.51, f32[512,512]{1,0:T(8,128)S(1)} %fusion.12, f32[512,512]{1,0:T(8,128)} %fusion.26, bf16[4,3,512,512]{3,2,1,0:T(8,128)(2,1)} %cw.1, ...), kind=kOutput, calls=%fused_computation.17 | convolution fusion | flops 272105472 | bytes 5376000 | tf_op jit(solution)/shard_map/dot_general | solution.py:411
  61.2 1.3 collective-permute-start.7
  62.5 6.2 %collective-permute-start.6 = (bf16[256,512]{1,0:T(8,128)(2,1)S(1)}, bf16[256,512]{1,0:T(8,128)(2,1)}, u32[]{:S(2)}, u32[]{:S(2)}) collective-permute-start(bf16[256,512]{1,0:T(8,128)(2,1)S(1)} %get-tuple-element.5), channel_id=1, source_target_pairs={{0,1},{1,2},{2,3},{4,5},{5,6},{6,7},{8,9},{9,10},{10,11},{12,13},{... | collective-permute-start | bytes 786440 | tf_op jit(solution)/shard_map/ppermute | solution.py:26
  70.3 1.5 fusion.22
  72.4 1.5 fusion.9
  73.9 2.8 %multiply_convert_fusion.1 = (bf16[512,512]{1,0:T(8,128)(2,1)S(1)}, f32[512,512]{1,0:T(8,128)}) fusion(bf16[512,512]{1,0:T(8,128)(2,1)S(1)} %get-tuple-element.16, f32[512]{0:T(512)S(1)} %fusion.51, f32[512,512]{1,0:T(8,128)S(1)} %fusion.9, f32[512,512]{1,0:T(8,128)S(1)} %fusion.22, bf16[4,3,512,512]{3,2,1,0:T(8,128)(2,1)} %cw.1, ...), kind=kOutput, calls=%fused_computation.16 | convolution fusion | flops 272105472 | bytes 5507072 | tf_op jit(solution)/shard_map/dot_general | solution.py:411
  76.9 8.0 %multiply_reduce_fusion = (f32[512]{0:T(512)S(1)}, f32[512,5120]{1,0:T(8,128)}) fusion(bf16[512,512]{1,0:T(8,128)(2,1)S(1)} %get-tuple-element.18, bf16[512,5120]{1,0:T(8,128)(2,1)} %hw.1), kind=kOutput, calls=%fused_computation.4 | convolution fusion | flops 2689596928 | bytes 16254976 | tf_op jit(solution)/shard_map/dot_general | solution.py:417
  86.1 6.2 %concatenate.80 = bf16[3520,4,2,64]{0,3,2,1:T(8,128)(2,1)} concatenate(bf16[32,4,2,64]{0,3,2,1:T(8,128)(2,1)S(1)} %bitcast.93, bf16[512,4,2,64]{0,3,2,1:T(8,128)(2,1)S(1)} %bitcast.86, bf16[32,4,2,64]{0,3,2,1:T(8,128)(2,1)} %bitcast.94, bf16[64,4,2,64]{0,3,2,1:T(8,128)(2,1)} %bitcast.95, bf16[512,4,2,64]{0,3,2,1:T(8,128)(2,1)S(1)} %bitcast.87, bf16[64,4,2,64]{0,3,2,1:T(8,128)(2,1)} %bitcast.96, ...), dimensions={0} | concatenate | bytes 7208960 | tf_op jit(solution)/shard_map/concatenate | solution.py:426
  92.4 3.6 %constant_dynamic-slice_fusion = (bf16[3520,4,1,64]{0,3,2,1:T(8,128)(2,1)S(1)}, bf16[3520,4,1,64]{0,3,2,1:T(8,128)(2,1)}) fusion(bf16[3520,4,2,64]{0,3,2,1:T(8,128)(2,1)} %concatenate.80, s32[]{:T(128)S(6)} %select_n.8, s32[]{:T(128)S(6)} %select_n.7), kind=kLoop, calls=%fused_computation.77 | loop fusion | bytes 7208968 | tf_op jit(solution)/shard_map/jit(dynamic_index_in_dim)/dynamic_slice | solution.py:430
  96.0 3.8 %copy.64.hid_mine = bf16[3520,256]{1,0:T(8,128)(2,1)} copy(bf16[3520,256]{0,1:T(8,128)(2,1)} %bitcast.83) | data formatting | bytes 3604480 | tf_op jit(solution)/shard_map/reshape | solution.py:430
  99.7 2.3 copy.65.hid_other
  102.0 6.9 %fusion = f32[512]{0:T(512)S(1)} fusion(f32[512,5120]{1,0:T(8,128)} %get-tuple-element.23, f32[512]{0:T(512)S(1)} %get-tuple-element.22), kind=kLoop, calls=%fused_computation.5 | loop fusion | flops 7863808 | bytes 10489856 | tf_op jit(solution)/shard_map/reduce_sum | solution.py:422
  108.9 13.0 %multiply_convert_fusion.gs = bf16[512,5120]{1,0:T(8,128)(2,1)} fusion(f32[512,5120]{1,0:T(8,128)} %get-tuple-element.23, f32[512,5120]{1,0:T(8,128)} %copy-done.2, f32[512]{0:T(512)S(1)} %fusion.2, f32[512]{0:T(512)S(1)} %get-tuple-element.20, f32[512]{0:T(512)S(1)} %fusion, f32[512]{0:T(512)S(1)} %get-tuple-element.22, f32[512]{0:T(512)S(1)} %fusion.50), kind=kLoop, calls=%fused_computation | loop fusion | flops 34078720 | bytes 26224640 | tf_op jit(solution)/shard_map/convert_element_type | solution.py:425
  122.0 119.2 %shard_map.77 = (f32[4,3,64,128]{3,2,1,0:T(8,128)}, f32[64,1280]{1,0:T(8,128)}) custom-call(bf16[3520,256]{1,0:T(8,128)(2,1)} %copy.64.hid_mine, bf16[3520,256]{1,0:T(8,128)(2,1)} %copy.65.hid_other, bf16[512,5120]{1,0:T(8,128)(2,1)} %multiply_convert_fusion.gs, bf16[512,5120]{1,0:T(8,128)(2,1)} %hw.1, bf16[4,3,512,512]{3,2,1,0:T(8,128)(2,1)} %cw.1, ...), custom_call_target="tpu_custom_call" | custom-call | tf_op jit(solution)/shard_map/pallas_call | solution.py:357
  241.2 1.8 copy.82
  242.9 1.7 copy.83
  (40 shorter events, 11.8 us)
Async XLA Ops:
  0.6 10.7 %copy-start = (bf16[1,512,768]{2,1,0:T(8,128)(2,1)S(1)}, bf16[1,512,768]{2,1,0:T(8,128)(2,1)}, u32[]{:S(2)}) copy-start(bf16[1,512,768]{2,1,0:T(8,128)(2,1)} %param.7) | copy-start | bytes 2359300
  1.5 23.8 %collective-permute-start.1 = (bf16[32,512]{1,0:T(8,128)(2,1)S(1)}, bf16[32,512]{1,0:T(8,128)(2,1)S(1)}, u32[]{:S(2)}, u32[]{:S(2)}) collective-permute-start(bf16[32,512]{1,0:T(8,128)(2,1)S(1)} %get-tuple-element.10), channel_id=1, source_target_pairs={{1,0},{2,1},{3,2},{5,4},{6,5},{7,6},{9,8},{10,9},{11,10},{13,12},{... | collective-permute-start | bytes 98312 | tf_op jit(solution)/shard_map/ppermute | solution.py:27
  2.8 24.0 %collective-permute-start = (bf16[32,512]{1,0:T(8,128)(2,1)S(1)}, bf16[32,512]{1,0:T(8,128)(2,1)S(1)}, u32[]{:S(2)}, u32[]{:S(2)}) collective-permute-start(bf16[32,512]{1,0:T(8,128)(2,1)S(1)} %get-tuple-element.11), channel_id=1, source_target_pairs={{0,1},{1,2},{2,3},{4,5},{5,6},{6,7},{8,9},{9,10},{10,11},{12,13},{... | collective-permute-start | bytes 98312 | tf_op jit(solution)/shard_map/ppermute | solution.py:26
  18.0 4.0 %copy-start.2 = (f32[512,5120]{1,0:T(8,128)}, f32[512,5120]{1,0:T(8,128)S(1)}, u32[]{:S(2)}) copy-start(f32[512,5120]{1,0:T(8,128)S(1)} %get-tuple-element.21) | copy-start | bytes 31457284
  18.1 7.0 %copy-start.3 = (bf16[1,512,512]{2,1,0:T(8,128)(2,1)S(1)}, bf16[1,512,512]{2,1,0:T(8,128)(2,1)}, u32[]{:S(2)}) copy-start(bf16[1,512,512]{2,1,0:T(8,128)(2,1)} %param.6) | copy-start | bytes 1572868
  25.3 4.3 %copy-start.4 = (bf16[32,512]{1,0:T(8,128)(2,1)}, bf16[32,512]{1,0:T(8,128)(2,1)S(1)}, u32[]{:S(2)}) copy-start(bf16[32,512]{1,0:T(8,128)(2,1)S(1)} %collective-permute-done.1) | copy-start | bytes 98308
  26.8 2.8 %copy-start.5 = (bf16[32,512]{1,0:T(8,128)(2,1)}, bf16[32,512]{1,0:T(8,128)(2,1)S(1)}, u32[]{:S(2)}) copy-start(bf16[32,512]{1,0:T(8,128)(2,1)S(1)} %collective-permute-done) | copy-start | bytes 98308
  29.5 10.9 %collective-permute-start.3 = (bf16[64,512]{1,0:T(8,128)(2,1)S(1)}, bf16[64,512]{1,0:T(8,128)(2,1)S(1)}, u32[]{:S(2)}, u32[]{:S(2)}) collective-permute-start(bf16[64,512]{1,0:T(8,128)(2,1)S(1)} %get-tuple-element.8), channel_id=1, source_target_pairs={{1,0},{2,1},{3,2},{5,4},{6,5},{7,6},{9,8},{10,9},{11,10},{13,12},{... | collective-permute-start | bytes 196616 | tf_op jit(solution)/shard_map/ppermute | solution.py:27
  32.5 9.3 %collective-permute-start.2 = (bf16[64,512]{1,0:T(8,128)(2,1)S(1)}, bf16[64,512]{1,0:T(8,128)(2,1)S(1)}, u32[]{:S(2)}, u32[]{:S(2)}) collective-permute-start(bf16[64,512]{1,0:T(8,128)(2,1)S(1)} %get-tuple-element.9), channel_id=1, source_target_pairs={{0,1},{1,2},{2,3},{4,5},{5,6},{6,7},{8,9},{9,10},{10,11},{12,13},{... | collective-permute-start | bytes 196616 | tf_op jit(solution)/shard_map/ppermute | solution.py:26
  44.6 11.0 %collective-permute-start.5 = (bf16[128,512]{1,0:T(8,128)(2,1)S(1)}, bf16[128,512]{1,0:T(8,128)(2,1)S(1)}, u32[]{:S(2)}, u32[]{:S(2)}) collective-permute-start(bf16[128,512]{1,0:T(8,128)(2,1)S(1)} %get-tuple-element.6), channel_id=1, source_target_pairs={{1,0},{2,1},{3,2},{5,4},{6,5},{7,6},{9,8},{10,9},{11,10},{13,12},{... | collective-permute-start | bytes 393224 | tf_op jit(solution)/shard_map/ppermute | solution.py:27
  48.7 8.5 %collective-permute-start.4 = (bf16[128,512]{1,0:T(8,128)(2,1)S(1)}, bf16[128,512]{1,0:T(8,128)(2,1)S(1)}, u32[]{:S(2)}, u32[]{:S(2)}) collective-permute-start(bf16[128,512]{1,0:T(8,128)(2,1)S(1)} %get-tuple-element.7), channel_id=1, source_target_pairs={{0,1},{1,2},{2,3},{4,5},{5,6},{6,7},{8,9},{9,10},{10,11},{12,13},{... | collective-permute-start | bytes 393224 | tf_op jit(solution)/shard_map/ppermute | solution.py:26
  61.2 11.1 %collective-permute-start.7 = (bf16[256,512]{1,0:T(8,128)(2,1)}, bf16[256,512]{1,0:T(8,128)(2,1)S(1)}, u32[]{:S(2)}, u32[]{:S(2)}) collective-permute-start(bf16[256,512]{1,0:T(8,128)(2,1)} %get-tuple-element.4), channel_id=1, source_target_pairs={{1,0},{2,1},{3,2},{5,4},{6,5},{7,6},{9,8},{10,9},{11,10},{13,12},{... | collective-permute-start | bytes 786440 | tf_op jit(solution)/shard_map/ppermute | solution.py:27
  62.5 11.3 %collective-permute-start.6 = (bf16[256,512]{1,0:T(8,128)(2,1)S(1)}, bf16[256,512]{1,0:T(8,128)(2,1)}, u32[]{:S(2)}, u32[]{:S(2)}) collective-permute-start(bf16[256,512]{1,0:T(8,128)(2,1)S(1)} %get-tuple-element.5), channel_id=1, source_target_pairs={{0,1},{1,2},{2,3},{4,5},{5,6},{6,7},{8,9},{9,10},{10,11},{12,13},{... | collective-permute-start | bytes 786440 | tf_op jit(solution)/shard_map/ppermute | solution.py:26
  122.0 122.7 %copy-start.1 = (bf16[1,512,768]{2,1,0:T(8,128)(2,1)S(1)}, bf16[1,512,768]{2,1,0:T(8,128)(2,1)}, u32[]{:S(2)}) copy-start(bf16[1,512,768]{2,1,0:T(8,128)(2,1)} %param.7) | copy-start | bytes 2359300

commit v2 on v1

--- a/solution.py
+++ b/solution.py
@@ -19,15 +19,6 @@
     return BASE_DILATION * 2**layer
 
 
-def extended(x, width):
-    devices, length = (lax.axis_size("tm"), x.shape[0])
-    up = [(i, (i + 1) % devices) for i in range(devices - 1)]
-    down = [(j, i) for i, j in up]
-    before = lax.ppermute(x[length - width :], "tm", up)
-    after = lax.ppermute(x[:width], "tm", down)
-    return jnp.concatenate([before, x, after], axis=0)
-
-
 def dot_tn(a, b):
     return lax.dot_general(a, b, (((0,), (0,)), ((), ())), preferred_element_type=F32)
 
@@ -39,8 +30,19 @@
 def backward_kernel(
     n_read,
     n_tm,
+    hid_mine_hbm,
+    hid_other,
+    gs_hbm,
+    hw_hbm,
+    cw_hbm,
+    pre0_hbm,
+    pre1_hbm,
+    pre2_hbm,
+    pre3_hbm,
+    mask,
+    out_conv,
+    out_head,
     hid_mine,
-    hid_other,
     gs,
     hw,
     cw,
@@ -48,9 +50,6 @@
     pre1,
     pre2,
     pre3,
-    mask,
-    out_conv,
-    out_head,
     hid_far,
     gs_far,
     grad,
@@ -62,10 +61,12 @@
     send_h,
     recv_h,
     acc_h,
+    done_h,
     last_h,
     send_c,
     recv_c,
     acc_c,
+    done_c,
     last_c,
     hid_sem,
     gs_sem,
@@ -73,6 +74,9 @@
     halo_sem,
     two_sem,
     three_sem,
+    gs_load_sem,
+    hw_load_sem,
+    load_sem,
 ):
     pres = (pre0, pre1, pre2, pre3)
     gpads = (gpad0, gpad1, gpad2, gpad3)
@@ -86,6 +90,24 @@
     sub = cols // HEAD_GROUPS
     r, t = lax.axis_index("read"), lax.axis_index("tm")
     core, q = lax.rem(r, 2), r // 2
+    step = scores // HEAD_GROUPS
+    gs_loads, hw_loads = [], []
+    for s in range(HEAD_GROUPS):
+        part = pl.ds(s * step, step)
+        for loads, far, near, sem in (
+            (gs_loads, gs_hbm, gs, gs_load_sem),
+            (hw_loads, hw_hbm, hw, hw_load_sem),
+        ):
+            loads.append(pltpu.make_async_copy(far.at[:, part], near.at[:, part], sem.at[s]))
+            loads[-1].start()
+    pre_hbm = (pre0_hbm, pre1_hbm, pre2_hbm, pre3_hbm)
+    pre_loads = [
+        pltpu.make_async_copy(pre_hbm[l], pres[l], load_sem.at[l]) for l in range(LAYERS)
+    ]
+    hid_load = pltpu.make_async_copy(hid_mine_hbm, hid_mine, load_sem.at[LAYERS])
+    cw_load = pltpu.make_async_copy(cw_hbm.at[pl.ds(1, LAYERS - 1)], cw, load_sem.at[LAYERS + 1])
+    for load in (pre_loads[3], hid_load, cw_load, pre_loads[2], pre_loads[1], pre_loads[0]):
+        load.start()
     twin = {"read": 2 * q + 1 - core}
     tm_peers = [{"tm": lax.rem(t + k, n_tm)} for k in range(1, n_tm)]
     q_next = [lax.rem(q + k, n_q) for k in range(1, n_q)]
@@ -122,7 +144,7 @@
             part = pl.ds(owner * cols + s * sub, sub)
             gs_copies.append(
                 start(
-                    gs.at[:, part],
+                    gs_hbm.at[:, part],
                     gs_far.at[:, part],
                     gs_sem.at[0, s, owner],
                     gs_sem.at[1, s, owner],
@@ -130,8 +152,9 @@
                 )
             )
 
-    step = scores // HEAD_GROUPS
     for s in range(HEAD_GROUPS):
+        gs_loads[s].wait()
+        hw_loads[s].wait()
         part = dot_nt(gs[:, s * step : (s + 1) * step], hw[:, s * step : (s + 1) * step])
         grad[...] = part if s == 0 else grad[...] + part
 
@@ -142,6 +165,7 @@
 
     def make_gpre(layer):
         d = reach(layer)
+        pre_loads[layer].wait()
         gpad, pre = gpads[layer], pres[layer][...]
         sigma = 1.0 / (1.0 + jnp.exp(-pre))
         g_act = mask[...] * grad[...]
@@ -191,7 +215,7 @@
     def back(layer):
         d = reach(layer)
         gpad = gpads[layer]
-        grad[...] = grad[...] + dot_nt(gpad[d : d + frames, :], cw[layer, 1])
+        grad[...] = grad[...] + dot_nt(gpad[d : d + frames, :], cw[layer - 1, 1])
         before, after = halos[layer]
 
         @pl.when(t < n_tm - 1)
@@ -202,8 +226,8 @@
         def _():
             after.wait_recv()
 
-        grad[...] = grad[...] + dot_nt(gpad[2 * d : 2 * d + frames, :], cw[layer, 0])
-        grad[...] = grad[...] + dot_nt(gpad[0:frames, :], cw[layer, 2])
+        grad[...] = grad[...] + dot_nt(gpad[2 * d : 2 * d + frames, :], cw[layer - 1, 0])
+        grad[...] = grad[...] + dot_nt(gpad[0:frames, :], cw[layer - 1, 2])
 
         @pl.when(t > 0)
         def _():
@@ -268,18 +292,20 @@
                 for slot in range(n_tm - 1):
                     total = total + recv_c[group, slot, k].astype(F32)
                 acc_c[group, k] = total
+                done_c[group, k] = total.astype(BF16)
         else:
             total = acc_h[group - LAYERS]
             for slot in range(n_tm - 1):
                 total = total + recv_h[group - LAYERS, slot].astype(F32)
             acc_h[group - LAYERS] = total
+            done_h[group - LAYERS] = total.astype(BF16)
         three[group] = []
         for k in range(1, n_q):
             part = pl.ds(pl.multiple_of(q_next[k - 1] * rows, rows), rows)
             if group < LAYERS:
-                src, dst = acc_c.at[group, :, part], last_c.at[group, k - 1]
+                src, dst = done_c.at[group, :, part], last_c.at[group, k - 1]
             else:
-                src, dst = acc_h.at[group - LAYERS, part], last_h.at[group - LAYERS, k - 1]
+                src, dst = done_h.at[group - LAYERS, part], last_h.at[group - LAYERS, k - 1]
             three[group].append(
                 start(
                     src,
@@ -298,19 +324,21 @@
             for k in range(3):
                 total = acc_c[group, k, part, :]
                 for slot in range(n_q - 1):
-                    total = total + last_c[group, slot, k]
+                    total = total + last_c[group, slot, k].astype(F32)
                 out_conv[group, k] = total
         else:
             s = group - LAYERS
             total = acc_h[s, part, :]
             for slot in range(n_q - 1):
-                total = total + last_h[s, slot]
+                total = total + last_h[s, slot].astype(F32)
             out_head[:, s * sub : (s + 1) * sub] = total
 
     make_gpre(3)
+    hid_load.wait()
     hid_copy.wait_recv()
     head(0)
     head(1)
+    cw_load.wait()
     back(3)
     make_gpre(2)
     head(2)
@@ -360,9 +388,16 @@
             jax.ShapeDtypeStruct((LAYERS, 3, rows, conv_cols), F32),
             jax.ShapeDtypeStruct((rows, cols), F32),
         ),
-        in_specs=[vmem] * 10,
+        in_specs=[pl.BlockSpec(memory_space=pl.ANY)] * 9 + [vmem],
         out_specs=(vmem, vmem),
         scratch_shapes=[
+            pltpu.VMEM(hid_mine.shape, BF16),
+            pltpu.VMEM(gs.shape, BF16),
+            pltpu.VMEM(hw.shape, BF16),
+            pltpu.VMEM((LAYERS - 1,) + cw.shape[1:], BF16),
+        ]
+        + [pltpu.VMEM((frames, width), F32)] * LAYERS
+        + [
             pltpu.VMEM(hid_mine.shape, BF16),
             pltpu.VMEM((frames, scores), BF16),
             pltpu.VMEM((frames, width), F32),
@@ -373,22 +408,181 @@
             pltpu.VMEM((HEAD_GROUPS, n_tm, half, sub), BF16),
             pltpu.VMEM((HEAD_GROUPS, n_tm - 1, half, sub), BF16),
             pltpu.VMEM((HEAD_GROUPS, half, sub), F32),
-            pltpu.VMEM((HEAD_GROUPS, n_q - 1, rows, sub), F32),
+            pltpu.VMEM((HEAD_GROUPS, half, sub), BF16),
+            pltpu.VMEM((HEAD_GROUPS, n_q - 1, rows, sub), BF16),
             pltpu.VMEM((LAYERS, n_tm, 3, half, conv_cols), BF16),
             pltpu.VMEM((LAYERS, n_tm - 1, 3, half, conv_cols), BF16),
             pltpu.VMEM((LAYERS, 3, half, conv_cols), F32),
-            pltpu.VMEM((LAYERS, n_q - 1, 3, rows, conv_cols), F32),
+            pltpu.VMEM((LAYERS, 3, half, conv_cols), BF16),
+            pltpu.VMEM((LAYERS, n_q - 1, 3, rows, conv_cols), BF16),
             dma((2,)),
             dma((2, HEAD_GROUPS, n_tm)),
             dma((2, LAYERS)),
             dma((2, 2, LAYERS)),
             dma((2, groups, n_tm - 1)),
             dma((2, groups, n_q - 1)),
+            dma((HEAD_GROUPS,)),
+            dma((HEAD_GROUPS,)),
+            dma((LAYERS + 2,)),
         ],
         compiler_params=pltpu.CompilerParams(
             collective_id=1, has_side_effects=True, vmem_limit_bytes=60 * 2**20
         ),
     )(hid_mine, hid_other, gs, hw, cw, *pres, mask)
+
+
+def forward_kernel(
+    n_read,
+    n_tm,
+    x,
+    cw_hbm,
+    mask,
+    out_mine,
+    out_other,
+    out_hidden,
+    pre0,
+    pre1,
+    pre2,
+    pre3,
+    hp0,
+    hp1,
+    hp2,
+    hp3,
+    cw,
+    cw_sem,
+    halo_sem,
+):
+    pres, pads = (pre0, pre1, pre2, pre3), (hp0, hp1, hp2, hp3)
+    frames, width = x.shape
+    half, rows = width // 2, width // n_read
+    r, t = lax.axis_index("read"), lax.axis_index("tm")
+    core = lax.rem(r, 2)
+    loads = [
+        pltpu.make_async_copy(cw_hbm.at[l], cw.at[l], cw_sem.at[l]) for l in range(LAYERS)
+    ]
+    for load in loads:
+        load.start()
+    hp0[reach(0) : reach(0) + frames, :] = x[...]
+
+    barrier = pltpu.get_barrier_semaphore()
+    for k in range(1, n_tm):
+        pl.semaphore_signal(
+            barrier, inc=1, device_id={"tm": lax.rem(t + k, n_tm)}, device_id_type=MESH
+        )
+    pl.semaphore_wait(barrier, n_tm - 1)
+
+    channel = lax.broadcasted_iota(jnp.int32, (width, half), 0)
+    place = lax.broadcasted_iota(jnp.int32, (width, half), 1)
+    wanted = 2 * rows * (place // rows) + lax.rem(place, rows)
+    pick_mine = (channel == wanted + rows * core).astype(F32).astype(BF16)
+    pick_other = (channel == wanted + rows * (1 - core)).astype(F32).astype(BF16)
+
+    def deal(value, at):
+        size = value.shape[0]
+        for out, pick in ((out_mine, pick_mine), (out_other, pick_other)):
+            out[at : at + size, :] = jnp.dot(
+                value, pick, preferred_element_type=F32
+            ).astype(BF16)
+
+    base = 0
+    for layer in range(LAYERS):
+        d = reach(layer)
+        pad = pads[layer]
+
+        def halo(side, first, landing, to, pad=pad, d=d, layer=layer):
+            return pltpu.make_async_remote_copy(
+                src_ref=pad.at[pl.ds(first, d)],
+                dst_ref=pad.at[pl.ds(landing, d)],
+                send_sem=halo_sem.at[side, 0, layer],
+                recv_sem=halo_sem.at[side, 1, layer],
+                device_id={"tm": lax.rem(t + to, n_tm)},
+                device_id_type=MESH,
+            )
+
+        before = halo(0, d, d + frames, n_tm - 1)
+        after = halo(1, frames, 0, 1)
+
+        @pl.when(t > 0)
+        def _():
+            before.start()
+
+        @pl.when(t < n_tm - 1)
+        def _():
+            after.start()
+
+        @pl.when(t == 0)
+        def _():
+            pad[0:d, :] = jnp.zeros((d, width), BF16)
+
+        @pl.when(t == n_tm - 1)
+        def _():
+            pad[d + frames : d + frames + d, :] = jnp.zeros((d, width), BF16)
+
+        loads[layer].wait()
+        pre = pres[layer]
+        pre[...] = jnp.dot(pad[d : d + frames, :], cw[layer, 1], preferred_element_type=F32)
+        deal(pad[d : d + frames, :], base + d)
+
+        @pl.when(t < n_tm - 1)
+        def _():
+            before.wait_recv()
+
+        @pl.when(t > 0)
+        def _():
+            after.wait_recv()
+
+        pre[...] += jnp.dot(pad[0:frames, :], cw[layer, 0], preferred_element_type=F32)
+        pre[...] += jnp.dot(
+            pad[2 * d : 2 * d + frames, :], cw[layer, 2], preferred_element_type=F32
+        )
+        total = pre[...]
+        hidden = (
+            mask[...]
+            * (pad[d : d + frames, :].astype(F32) + total * (1.0 / (1.0 + jnp.exp(-total))))
+        ).astype(BF16)
+        if layer < LAYERS - 1:
+            pads[layer + 1][2 * d : 2 * d + frames, :] = hidden
+        else:
+            out_hidden[...] = hidden
+        deal(pad[0:d, :], base)
+        deal(pad[d + frames : d + frames + d, :], base + d + frames)
+
+        @pl.when(t > 0)
+        def _():
+            before.wait_send()
+
+        @pl.when(t < n_tm - 1)
+        def _():
+            after.wait_send()
+
+        base += frames + 2 * d
+    deal(out_hidden[...], base)
+
+
+def forward(x, cw, mask):
+    n_read, n_tm = lax.axis_size("read"), lax.axis_size("tm")
+    frames, width = x.shape
+    total = frames + sum(frames + 2 * reach(l) for l in range(LAYERS))
+    vmem = pl.BlockSpec(memory_space=pltpu.VMEM)
+    dma = pltpu.SemaphoreType.DMA
+    return pl.pallas_call(
+        functools.partial(forward_kernel, n_read, n_tm),
+        out_shape=[
+            jax.ShapeDtypeStruct((total, width // 2), BF16),
+            jax.ShapeDtypeStruct((total, width // 2), BF16),
+            jax.ShapeDtypeStruct((frames, width), BF16),
+        ]
+        + [jax.ShapeDtypeStruct((frames, width), F32)] * LAYERS,
+        in_specs=[vmem, pl.BlockSpec(memory_space=pl.ANY), vmem],
+        out_specs=[vmem] * (3 + LAYERS),
+        scratch_shapes=[
+            pltpu.VMEM((frames + 2 * reach(l), width), BF16) for l in range(LAYERS)
+        ]
+        + [pltpu.VMEM(cw.shape, BF16), dma((LAYERS,)), dma((2, 2, LAYERS))],
+        compiler_params=pltpu.CompilerParams(
+            collective_id=0, has_side_effects=True, vmem_limit_bytes=48 * 2**20
+        ),
+    )(x, cw, mask)
 
 
 def on_device(student_in, teacher_rows, valid, conv_weight, head_weight, teacher_head_weight):
@@ -401,19 +595,7 @@
     first_frame = lax.axis_index("tm") * frames
     positions = first_frame + jnp.arange(frames, dtype=jnp.int32)
     mask = (positions < valid[0]).astype(F32)[:, None]
-    hidden = student_in[0]
-    pads, pres = [], []
-    for layer in range(LAYERS):
-        d = reach(layer)
-        padded = extended(hidden, d)
-        pre = jnp.zeros((frames, width), F32)
-        for k in range(3):
-            pre = pre + jnp.dot(
-                padded[k * d : k * d + frames], conv_weight[layer, k], preferred_element_type=F32
-            )
-        pads.append(padded)
-        pres.append(pre)
-        hidden = (mask * (hidden.astype(F32) + jax.nn.silu(pre))).astype(BF16)
+    mine, other, hidden, *pres = forward(student_in[0], conv_weight, mask)
     squash = jnp.tanh(jnp.dot(hidden, head_weight, preferred_element_type=F32))
     teacher = 5.0 * jnp.tanh(
         jnp.dot(teacher_rows[0], teacher_head_weight, preferred_element_type=F32)
@@ -423,13 +605,6 @@
     g_score = (
         loss_scale * mask * (prob_student - prob_teacher) * 5.0 * (1.0 - squash * squash)
     ).astype(BF16)
-    every = jnp.concatenate(pads + [hidden], axis=0)
-    every = every.reshape(every.shape[0], n_read // 2, 2, width // n_read)
-    core = lax.rem(lax.axis_index("read"), 2)
-    mine, other = (
-        lax.dynamic_index_in_dim(every, which, 2, keepdims=False).reshape(-1, width // 2)
-        for which in (core, 1 - core)
-    )
     return backward(mine, other, g_score, head_weight, conv_weight, pres, mask)
 
 

time: 246 us -> 163 us (0.66)
  local copies, waits for them, and re-layouts: 32.7 us -> 4.56 us
  matrix products: 39.1 us -> 11.2 us
  starting transfers between devices: 27.7 us -> 0 us
  Pallas kernels: 119 us -> 129 us
  other arithmetic: 23.7 us -> 16.2 us
    pallas_call x0 -> x1, Pallas kernels: none -> 30.2 us  [forward(): pl.pallas_call(functools.partial(forward_kernel, n_read, n_tm), out_shape...]
    ppermute x8 -> x0, starting transfers between devices: 27.7 us -> none  [the longest x4 22.6 us: extended(): before = lax.ppermute(x[length - width:], 'tm', up)]
    dot_general x12 -> x0, matrix products: 24.4 us -> none  [on_device(): jnp.dot(padded[k * d:k * d + frames], conv_weight[layer, k], preferred_el...]
    pallas_call x1, Pallas kernels: 119 us -> 98.4 us  [backward(): pl.pallas_call(functools.partial(backward_kernel, n_read, n_tm), out_shap...]
    concatenate x5 -> x0, local copies, waits for them, and re-layouts: 10.1 us -> none  [on_device(): every = jnp.concatenate(pads + [hidden], axis=0)]
    reshape x2 -> x0, local copies, waits for them, and re-layouts: 6.04 us -> none  [on_device(): lax.dynamic_index_in_dim(every, which, 2, keepdims=False)]
    dynamic_slice x1 -> x0, local copies, waits for them, and re-layouts: 3.61 us -> none  [on_device(): lax.dynamic_index_in_dim(every, which, 2, keepdims=False)]
    convert_element_type x1, other arithmetic: 13 us -> 9.81 us  [on_device(): g_score = (loss_scale * mask * (prob_student - prob_teacher) * 5.0 * (1.0...]
  transfers between devices with their start and end apart: 8 -> 0, of which waited for: 1 -> 0; matrix products, arithmetic and copies ran while one was open for 12% -> 0% of each run, Pallas kernels for 0% -> 0%
where the time goes in v2:
time: 163 us; the launch traced here: 162 us
  Pallas kernels  129 us (79%)
  other arithmetic  16.2 us (10%)
  matrix products  11.2 us (7%)
  local copies, waits for them, and re-layouts  4.56 us (3%)
    pallas_call x1, Pallas kernels, backward(): pl.pallas_call(functools.partial(backward_kernel, n_read, n_tm), out_shap...  98.4 us
    pallas_call x1, Pallas kernels, forward(): pl.pallas_call(functools.partial(forward_kernel, n_read, n_tm), out_shape...  30.2 us
    convert_element_type x1, other arithmetic, on_device(): g_score = (loss_scale * mask * (prob_student - prob_teacher) * 5.0 * (1.0...  9.81 us
    dot_general x1, matrix products, on_device(): squash = jnp.tanh(jnp.dot(hidden, head_weight, preferred_element_type=F32))  6.78 us
    reduce_sum x1, other arithmetic, on_device(): prob_student = jax.nn.softmax(5.0 * squash, axis=-1)  6.32 us
    unnamed x20, local copies, waits for them, and re-layouts  4.56 us
    dot_general x1, matrix products, on_device(): jnp.dot(teacher_rows[0], teacher_head_weight, preferred_element_type=F32)  4.41 us

profile of v2, /device:TPU:0, one launch (start us, length us, event | category | flops | bytes accessed | tf_op | source)
XLA Modules:
  0.0 162.0 jit_solution(2291455644220899031)
XLA Ops:
  0.6 0.0 copy-start
  1.4 0.0 copy-start.6
  1.4 1.0 copy-done.6
  2.5 0.0 copy-start.1
  2.5 30.2 %shard_map.77 = (bf16[3520,256]{1,0:T(8,128)(2,1)}, bf16[3520,256]{1,0:T(8,128)(2,1)}, bf16[512,512]{1,0:T(8,128)(2,1)S(1)}, f32[512,512]{1,0:T(8,128)S(1)}, f32...) custom-call(bf16[512,512]{1,0:T(8,128)(2,1)S(1)} %bitcast.12, ...), custom_call_target="tpu_custom_call" | custom-call | tf_op jit(solution)/shard_map/pallas_call | solution.py:568
  32.6 0.0 copy-start.2
  32.7 0.0 copy-start.3
  32.7 0.0 copy-start.4
  32.7 0.0 copy-start.5
  32.7 0.0 slice-start
  32.7 0.0 slice-start.1
  32.7 6.8 %multiply_reduce_fusion = (f32[512]{0:T(512)S(1)}, f32[512,5120]{1,0:T(8,128)S(1)}) fusion(bf16[512,512]{1,0:T(8,128)(2,1)S(1)} %get-tuple-element.11, bf16[512,5120]{1,0:T(8,128)(2,1)} %hw_hbm.1), kind=kOutput, calls=%fused_computation.4 | convolution fusion | flops 2689596928 | bytes 16254976 | tf_op jit(solution)/shard_map/dot_general | solution.py:599
  39.5 0.0 copy-done.1
  39.5 0.0 copy-done
  39.5 0.0 slice-done
  39.5 0.0 slice-done.1
  39.5 4.4 %fusion.1 = (f32[512]{0:T(512)S(1)}, f32[512,5120]{1,0:T(8,128)S(1)}) fusion(bf16[768,5120]{1,0:T(8,128)(2,1)S(1)} %bitcast.14, bf16[1,512,768]{2,1,0:T(8,128)(2,1)S(1)} %copy-done), kind=kOutput, calls=%fused_computation.6 | convolution fusion | flops 4031774208 | bytes 19138560 | tf_op jit(solution)/shard_map/dot_general | solution.py:601
  44.0 0.0 copy-done.2
  44.0 0.0 copy-done.3
  44.0 0.0 copy-done.4
  44.0 0.0 copy-done.5
  44.0 6.3 %fusion = (f32[512]{0:T(512)S(1)}, f32[512]{0:T(512)S(1)}) fusion(f32[512,5120]{1,0:T(8,128)S(1)} %get-tuple-element.19, f32[512]{0:T(512)S(1)} %get-tuple-element.18, f32[512]{0:T(512)S(1)} %get-tuple-element.16, f32[512,5120]{1,0:T(8,128)S(1)} %get-tuple-element.17), kind=kLoop, calls=%fused_computation.5 | loop fusion | flops 15727616 | bytes 20979712 | tf_op jit(solution)/shard_map/reduce_sum | solution.py:604
  50.3 9.8 %multiply_convert_fusion.gs_hbm = bf16[512,5120]{1,0:T(8,128)(2,1)} fusion(f32[512,5120]{1,0:T(8,128)S(1)} %get-tuple-element.19, f32[512,5120]{1,0:T(8,128)S(1)} %get-tuple-element.17, f32[512]{0:T(512)S(1)} %get-tuple-element.21, f32[512]{0:T(512)S(1)} %get-tuple-element.16, f32[512]{0:T(512)S(1)} %get-tuple-element.20, f32[512]{0:T(512)S(1)} %get-tuple-element.18, ...), kind=kLoop, calls=%fused_computation | loop fusion | flops 34078720 | bytes 26224640 | tf_op jit(solution)/shard_map/convert_element_type | solution.py:607
  60.1 98.4 %shard_map.78 = (f32[4,3,64,128]{3,2,1,0:T(8,128)}, f32[64,1280]{1,0:T(8,128)}) custom-call(bf16[3520,256]{1,0:T(8,128)(2,1)} %get-tuple-element.9.hid_mine_hbm, bf16[3520,256]{1,0:T(8,128)(2,1)} %get-tuple-element.10.hid_other, bf16[512,5120]{1,0:T(8,128)(2,1)} %multiply_convert_fusion.gs_hbm, bf16[512,5120]{1,0:T(8,128)(2,1)} %hw_hbm.1, ...), custom_call_target="tpu_custom_call" | custom-call | tf_op jit(solution)/shard_map/pallas_call | solution.py:385
  158.5 1.8 %copy.11 = f32[4,3,64,128]{3,2,1,0:T(8,128)} copy(f32[4,3,64,128]{3,2,1,0:T(8,128)} %get-tuple-element.24) | data formatting | bytes 786432
  160.3 1.7 %copy.12 = f32[64,1280]{1,0:T(8,128)} copy(f32[64,1280]{1,0:T(8,128)} %get-tuple-element.25) | data formatting | bytes 655360
  (3 shorter events, 0.0 us)
Async XLA Ops:
  0.6 38.9 %copy-start = (bf16[1,512,768]{2,1,0:T(8,128)(2,1)S(1)}, bf16[1,512,768]{2,1,0:T(8,128)(2,1)}, u32[]{:S(2)}) copy-start(bf16[1,512,768]{2,1,0:T(8,128)(2,1)} %param.7) | copy-start | bytes 2359300
  1.4 1.0 copy-start.6
  2.5 37.0 %copy-start.1 = (f32[512,1]{1,0:T(8,128)}, f32[512,1]{1,0:T(8,128)S(1)}, u32[]{:S(2)}) copy-start(f32[512,1]{1,0:T(8,128)S(1)} %fusion.5.mask) | copy-start | bytes 6148
  32.6 11.3 %copy-start.2 = (f32[512,512]{1,0:T(8,128)}, f32[512,512]{1,0:T(8,128)S(1)}, u32[]{:S(2)}) copy-start(f32[512,512]{1,0:T(8,128)S(1)} %get-tuple-element.12.pre0_hbm) | copy-start | bytes 3145732
  32.7 11.3 %copy-start.3 = (f32[512,512]{1,0:T(8,128)}, f32[512,512]{1,0:T(8,128)S(1)}, u32[]{:S(2)}) copy-start(f32[512,512]{1,0:T(8,128)S(1)} %get-tuple-element.13.pre1_hbm) | copy-start | bytes 3145732
  32.7 11.3 %copy-start.4 = (f32[512,512]{1,0:T(8,128)}, f32[512,512]{1,0:T(8,128)S(1)}, u32[]{:S(2)}) copy-start(f32[512,512]{1,0:T(8,128)S(1)} %get-tuple-element.14.pre2_hbm) | copy-start | bytes 3145732
  32.7 11.3 %copy-start.5 = (f32[512,512]{1,0:T(8,128)}, f32[512,512]{1,0:T(8,128)S(1)}, u32[]{:S(2)}) copy-start(f32[512,512]{1,0:T(8,128)S(1)} %get-tuple-element.15.pre3_hbm) | copy-start | bytes 3145732
  32.7 6.8 %slice-start = ((s8[7864320]{0:T(1024)(128)(4,1)}), s8[4194304]{0:T(1024)(128)(4,1)S(1)}, s32[]{:S(2)}) async-start(s8[7864320]{0:T(1024)(128)(4,1)} %bitcast.13), calls=%async_computation | async-start | bytes 8388608
  32.7 6.8 %slice-start.1 = ((s8[7864320]{0:T(1024)(128)(4,1)}), s8[3670016]{0:T(1024)(128)(4,1)S(1)}, s32[]{:S(2)}) async-start(s8[7864320]{0:T(1024)(128)(4,1)} %bitcast.13), calls=%async_computation.1 | async-start | bytes 7340032

commit v3 on v2

--- a/solution.py
+++ b/solution.py
@@ -152,11 +152,11 @@
                 )
             )
 
-    for s in range(HEAD_GROUPS):
-        gs_loads[s].wait()
-        hw_loads[s].wait()
-        part = dot_nt(gs[:, s * step : (s + 1) * step], hw[:, s * step : (s + 1) * step])
-        grad[...] = part if s == 0 else grad[...] + part
+    def head_back():
+        for s in range(HEAD_GROUPS):
+            hw_loads[s].wait()
+            part = dot_nt(gs[:, s * step : (s + 1) * step], hw[:, s * step : (s + 1) * step])
+            grad[...] = part if s == 0 else grad[...] + part
 
     gp_copies = {}
     two = {}
@@ -333,40 +333,44 @@
                 total = total + last_h[s, slot].astype(F32)
             out_head[:, s * sub : (s + 1) * sub] = total
 
-    make_gpre(3)
+    for load in gs_loads:
+        load.wait()
     hid_load.wait()
     hid_copy.wait_recv()
     head(0)
     head(1)
+    head_back()
+    make_gpre(3)
+    head(2)
     cw_load.wait()
     back(3)
     make_gpre(2)
-    head(2)
-    head(3)
+    conv(3)
     back(2)
     make_gpre(1)
-    head(4)
-    conv(3)
+    conv(2)
     finish_two(4)
     back(1)
     make_gpre(0)
-    conv(2)
+    conv(1)
     finish_two(5)
-    conv(1)
+    conv(0)
+    head(3)
+    head(4)
     finish_two(6)
-    conv(0)
-    finish_two(7)
-    finish_two(8)
     finish_three(4)
     finish_two(3)
     finish_three(5)
     finish_two(2)
     finish_three(6)
-    finish_three(7)
     finish_two(1)
-    finish_three(8)
+    finish_three(3)
     finish_two(0)
-    for group in (3, 2, 1, 0):
+    finish_three(2)
+    finish_two(7)
+    finish_three(1)
+    finish_two(8)
+    for group in (0, 7, 8):
         finish_three(group)
     for copy in sent:
         copy.wait_send()
@@ -600,8 +604,9 @@
     teacher = 5.0 * jnp.tanh(
         jnp.dot(teacher_rows[0], teacher_head_weight, preferred_element_type=F32)
     )
-    prob_teacher = jax.nn.softmax(teacher, axis=-1)
-    prob_student = jax.nn.softmax(5.0 * squash, axis=-1)
+    exp_teacher, exp_student = jnp.exp(teacher), jnp.exp(5.0 * squash)
+    prob_teacher = exp_teacher * (1.0 / jnp.sum(exp_teacher, axis=-1, keepdims=True))
+    prob_student = exp_student * (1.0 / jnp.sum(exp_student, axis=-1, keepdims=True))
     g_score = (
         loss_scale * mask * (prob_student - prob_teacher) * 5.0 * (1.0 - squash * squash)
     ).astype(BF16)

time: 163 us -> 160 us (0.982)
  other arithmetic: 16.2 us -> 8.9 us
  Pallas kernels: 129 us -> 132 us
  matrix products: 11.2 us -> 13.1 us
    reduce_sum x1 -> x0, other arithmetic: 6.32 us -> none  [on_device(): prob_student = jax.nn.softmax(5.0 * squash, axis=-1)]
    pallas_call x1, Pallas kernels: 98.4 us -> 102 us  [backward(): pl.pallas_call(functools.partial(backward_kernel, n_read, n_tm), out_shap...]
where the time goes in v3:
time: 160 us
  Pallas kernels  132 us (82%)
  matrix products  13.1 us (8%)
  other arithmetic  8.9 us (6%)
  local copies, waits for them, and re-layouts  4.56 us (3%)
    pallas_call x1, Pallas kernels, backward(): pl.pallas_call(functools.partial(backward_kernel, n_read, n_tm), out_shap...  102 us
    pallas_call x1, Pallas kernels, forward(): pl.pallas_call(functools.partial(forward_kernel, n_read, n_tm), out_shape...  30.2 us
    convert_element_type x1, other arithmetic, on_device(): g_score = (loss_scale * mask * (prob_student - prob_teacher) * 5.0 * (1.0...  8.85 us
    dot_general x1, matrix products, on_device(): squash = jnp.tanh(jnp.dot(hidden, head_weight, preferred_element_type=F32))  7.58 us
    dot_general x1, matrix products, on_device(): jnp.dot(teacher_rows[0], teacher_head_weight, preferred_element_type=F32)  5.49 us
    unnamed x20, local copies, waits for them, and re-layouts  4.56 us

profile of v3, /device:TPU:0, one launch (start us, length us, event | category | flops | bytes accessed | tf_op | source)
XLA Modules:
  0.0 160.0 jit_solution(3537532223251564380)
XLA Ops:
  0.6 0.0 copy-start
  1.4 0.0 copy-start.6
  1.4 1.0 copy-done.6
  2.5 0.0 copy-start.1
  2.5 30.2 %shard_map.77 = (bf16[3520,256]{1,0:T(8,128)(2,1)}, bf16[3520,256]{1,0:T(8,128)(2,1)}, bf16[512,512]{1,0:T(8,128)(2,1)S(1)}, f32[512,512]{1,0:T(8,128)S(1)}, f32...) custom-call(bf16[512,512]{1,0:T(8,128)(2,1)S(1)} %bitcast.12, ...), custom_call_target="tpu_custom_call" | custom-call | tf_op jit(solution)/shard_map/pallas_call | solution.py:572
  32.6 0.0 copy-start.2
  32.6 0.0 copy-start.3
  32.7 0.0 copy-start.4
  32.7 0.0 copy-start.5
  32.7 0.0 slice-start
  32.7 0.0 slice-start.1
  32.7 7.6 %fusion = (f32[512]{0:T(512)S(1)}, f32[512,5120]{1,0:T(8,128)S(1)}) fusion(bf16[512,512]{1,0:T(8,128)(2,1)S(1)} %get-tuple-element.11, bf16[512,5120]{1,0:T(8,128)(2,1)} %hw_hbm.1), kind=kOutput, calls=%fused_computation.3 | convolution fusion | flops 2689596928 | bytes 16254976 | tf_op jit(solution)/shard_map/dot_general | solution.py:603
  40.3 0.0 copy-done.1
  40.3 0.0 copy-done
  40.3 0.0 slice-done
  40.3 0.0 slice-done.1
  40.4 5.5 %fusion.1 = (f32[512]{0:T(512)S(1)}, f32[512,5120]{1,0:T(8,128)S(1)}) fusion(bf16[768,5120]{1,0:T(8,128)(2,1)S(1)} %bitcast.14, bf16[1,512,768]{2,1,0:T(8,128)(2,1)S(1)} %copy-done), kind=kOutput, calls=%fused_computation.4 | convolution fusion | flops 4031774208 | bytes 19138560 | tf_op jit(solution)/shard_map/dot_general | solution.py:605
  45.8 0.0 copy-done.2
  45.8 0.0 copy-done.3
  45.9 0.0 copy-done.4
  45.9 0.0 copy-done.5
  45.9 8.8 %multiply_convert_fusion.gs_hbm = bf16[512,5120]{1,0:T(8,128)(2,1)} fusion(f32[512,5120]{1,0:T(8,128)S(1)} %get-tuple-element.19, f32[512,5120]{1,0:T(8,128)S(1)} %get-tuple-element.17, f32[512]{0:T(512)S(1)} %get-tuple-element.21, f32[512]{0:T(512)S(1)} %broadcast_divide_fusion.1, f32[512]{0:T(512)S(1)} %get-tuple-element.20), kind=kLoop, calls=%fused_computation | loop fusion | flops 28835840 | bytes 26220544 | tf_op jit(solution)/shard_map/convert_element_type | solution.py:612
  54.7 101.8 %shard_map.78 = (f32[4,3,64,128]{3,2,1,0:T(8,128)}, f32[64,1280]{1,0:T(8,128)}) custom-call(bf16[3520,256]{1,0:T(8,128)(2,1)} %get-tuple-element.9.hid_mine_hbm, bf16[3520,256]{1,0:T(8,128)(2,1)} %get-tuple-element.10.hid_other, bf16[512,5120]{1,0:T(8,128)(2,1)} %multiply_convert_fusion.gs_hbm, bf16[512,5120]{1,0:T(8,128)(2,1)} %hw_hbm.1, ...), custom_call_target="tpu_custom_call" | custom-call | tf_op jit(solution)/shard_map/pallas_call | solution.py:389
  156.5 1.8 %copy.11 = f32[4,3,64,128]{3,2,1,0:T(8,128)} copy(f32[4,3,64,128]{3,2,1,0:T(8,128)} %get-tuple-element.24) | data formatting | bytes 786432
  158.3 1.7 %copy.12 = f32[64,1280]{1,0:T(8,128)} copy(f32[64,1280]{1,0:T(8,128)} %get-tuple-element.25) | data formatting | bytes 655360
  (4 shorter events, 0.1 us)
Async XLA Ops:
  0.6 39.7 %copy-start = (bf16[1,512,768]{2,1,0:T(8,128)(2,1)S(1)}, bf16[1,512,768]{2,1,0:T(8,128)(2,1)}, u32[]{:S(2)}) copy-start(bf16[1,512,768]{2,1,0:T(8,128)(2,1)} %param.7) | copy-start | bytes 2359300
  1.4 1.0 copy-start.6
  2.5 37.8 %copy-start.1 = (f32[512,1]{1,0:T(8,128)}, f32[512,1]{1,0:T(8,128)S(1)}, u32[]{:S(2)}) copy-start(f32[512,1]{1,0:T(8,128)S(1)} %fusion.4.mask) | copy-start | bytes 6148
  32.6 13.2 %copy-start.2 = (f32[512,512]{1,0:T(8,128)}, f32[512,512]{1,0:T(8,128)S(1)}, u32[]{:S(2)}) copy-start(f32[512,512]{1,0:T(8,128)S(1)} %get-tuple-element.12.pre0_hbm) | copy-start | bytes 3145732
  32.6 13.2 %copy-start.3 = (f32[512,512]{1,0:T(8,128)}, f32[512,512]{1,0:T(8,128)S(1)}, u32[]{:S(2)}) copy-start(f32[512,512]{1,0:T(8,128)S(1)} %get-tuple-element.13.pre1_hbm) | copy-start | bytes 3145732
  32.7 13.2 %copy-start.4 = (f32[512,512]{1,0:T(8,128)}, f32[512,512]{1,0:T(8,128)S(1)}, u32[]{:S(2)}) copy-start(f32[512,512]{1,0:T(8,128)S(1)} %get-tuple-element.14.pre2_hbm) | copy-start | bytes 3145732
  32.7 13.2 %copy-start.5 = (f32[512,512]{1,0:T(8,128)}, f32[512,512]{1,0:T(8,128)S(1)}, u32[]{:S(2)}) copy-start(f32[512,512]{1,0:T(8,128)S(1)} %get-tuple-element.15.pre3_hbm) | copy-start | bytes 3145732
  32.7 7.7 %slice-start = ((s8[7864320]{0:T(1024)(128)(4,1)}), s8[4194304]{0:T(1024)(128)(4,1)S(1)}, s32[]{:S(2)}) async-start(s8[7864320]{0:T(1024)(128)(4,1)} %bitcast.13), calls=%async_computation | async-start | bytes 8388608
  32.7 7.6 %slice-start.1 = ((s8[7864320]{0:T(1024)(128)(4,1)}), s8[3670016]{0:T(1024)(128)(4,1)S(1)}, s32[]{:S(2)}) async-start(s8[7864320]{0:T(1024)(128)(4,1)} %bitcast.13), calls=%async_computation.1 | async-start | bytes 7340032
